TPU v7x, 32 devices: a whole 2x2x4 slice. The times are simulated.
32 devices in a mesh: rep: 2 (over x), row: 16 (over z, y, core).
Axes of the slice: x: 2, y: 2, z: 4, core: 2. Of those that a mesh axis runs over, the one named last changes fastest.
Arguments:
- grad_out: bfloat16 [4096, 256], P(('rep', 'row')), may hold values from -6 to 6
- relu_mask: int32 [4096, 256], P(('rep', 'row')), may hold values 0 or 1
- layer_input: bfloat16 [4096, 256], P(('rep', 'row')), may hold values from -6 to 6
- weight: bfloat16 [256, 256], replicated, may hold values from -0.375 to 0.375
- tile_values: bfloat16 [4096, 128, 128], P(('rep', 'row')), may hold values from -0.0625 to 0.0625
- tile_rows: int32 [4096], P(('rep', 'row')), may hold values from 0 to 1
- tile_cols: int32 [4096], P(('rep', 'row')), may hold values from 0 to 15
- tile_count: int32 [32], P(('rep', 'row')), may hold values from 32 to 128, as said below
Outputs:
- grad_input: bfloat16 [4096, 256], P(('rep', 'row'))
- grad_weight: float32 [256, 256], replicated
Inputs may be any that keep to these rules, and one draw needn't show every extreme that they name: Slots k < tile_count[d] of device d are live; some device has 128 live slots; two devices whose indices differ only in the lowest bit hold together at most 160 live slots, and some such pair reaches it.
All inputs are finite; a program needn't handle non-finite values. No bound on the sum of `relu_mask` on one device may be relied on, other than what follows from the above.
Results may differ from a plain program's by a relative error of at most 0.015.
Values may be sent and summed in bfloat16 or wider, within the bound.
No kernel may reach another device: no remote copies, remote signals or barrier semaphores. Data moves between devices by JAX's collectives and lax.ppermute only.
A program may use at most 64 MiB of HBM per device.

v0:
```python
import jax
import jax.numpy as jnp
from jax import lax
from jax.sharding import PartitionSpec as P

slot_group = 8


def tile_pass(values, rows_ids, cols_ids, live_count, sources, out_blocks):
    block_rows = values.shape[1]
    features = sources.shape[2]
    slot_total = values.shape[0]

    def one_turn(turn_id, totals):
        slot_ids = turn_id * slot_group + jnp.arange(slot_group, dtype=jnp.int32)
        alive_mask = slot_ids < live_count
        clipped = jnp.minimum(slot_ids, slot_total - 1)
        tile_block = values[clipped]
        picked = sources[cols_ids[clipped]]
        products = jnp.einsum(
            "kab,kbf->kaf", tile_block, picked, preferred_element_type=jnp.float32
        )
        onehot = (
            rows_ids[clipped][None, :] == jnp.arange(out_blocks, dtype=jnp.int32)[:, None]
        ) & alive_mask[None, :]
        return totals + jnp.einsum("rk,kaf->raf", onehot.astype(jnp.float32), products)

    turn_count = (live_count + slot_group - 1) // slot_group
    start_totals = jnp.zeros((out_blocks, block_rows, features), jnp.float32)
    return lax.fori_loop(0, turn_count, one_turn, start_totals)


def body(grad_out, relu_mask, layer_input, weight, tile_values, tile_rows, tile_cols, tile_count):
    block_rows = tile_values.shape[1]
    features = grad_out.shape[1]
    out_blocks = lax.axis_size("rep")
    nodes_total = block_rows * lax.axis_size("rep") * lax.axis_size("row")
    masked = grad_out * relu_mask.astype(jnp.bfloat16)
    group_rows = lax.all_gather(masked, "row", axis=0, tiled=True)
    sources = group_rows.reshape(-1, block_rows, features)
    live_count = tile_count[0]
    partial_value = tile_pass(tile_values, tile_rows, tile_cols, live_count, sources, out_blocks)
    partial_value = partial_value.reshape(out_blocks * block_rows, features)
    owned = lax.psum_scatter(partial_value, "rep", scatter_dimension=0, tiled=True)
    prop_rounded = owned.astype(jnp.bfloat16)
    grad_input = lax.dot_general(
        prop_rounded, weight, (((1,), (1,)), ((), ())), preferred_element_type=jnp.float32
    ).astype(jnp.bfloat16)
    local_terms = lax.dot_general(
        layer_input, prop_rounded, (((0,), (0,)), ((), ())), preferred_element_type=jnp.float32
    )
    grad_weight = lax.psum(local_terms, ("rep", "row")) * (1.0 / nodes_total**0.5)
    return (grad_input, grad_weight)


def solution(mesh):
    placed = (
        P(("rep", "row"), None),
        P(("rep", "row"), None),
        P(("rep", "row"), None),
        P(),
        P(("rep", "row"), None, None),
        P(("rep", "row")),
        P(("rep", "row")),
        P(("rep", "row")),
    )
    return jax.shard_map(
        body, mesh=mesh, in_specs=placed, out_specs=(P(("rep", "row"), None), P()), check_vma=False
    )
```

profile of v0, /device:TPU:0, one launch (start us, length us, event | category | flops | bytes accessed | tf_op | source)
XLA Modules:
  0.0 344.8 jit_solution(17956802654649172469)
XLA Ops:
  9.6 41.8 %all-gather.2.cloned.1.call-done = bf16[2048,256]{1,0:T(8,128)(2,1)} async-done(((bf16[128,256]{1,0:T(8,128)(2,1)}), bf16[2048,256]{1,0:T(8,128)(2,1)}) %all-gather.2.cloned.1.call-update) | async-done | bytes 1048592 | tf_op jit(solution)/shard_map/all_gather | solution.py:39
  51.5 124.7 %while.10 = (s32[]{:T(128)}, f32[2,128,256]{2,0,1:T(2,128)S(1)}, s32[]{:T(128)}, s32[128]{0:T(128)}, s32[]{:T(128)}, /*index=5*/bf16[128,128,128]{2,1,0:T(8,128)...) while((s32[]{:T(128)}, f32[2,128,256]{2,0,1:T(2,128)S(1)}, s32[]{:T(128)}, ...), condition=%wide.region_1.2_spmd, body=%wide.region_0.1_spmd.sunk | while | flops 68225136 | bytes 3940941 | solution.py:30
  54.8 2.8 gather_fusion
  57.6 1.8 gather_fusion.2
  63.7 2.8 gather_fusion
  66.5 1.8 gather_fusion.2
  72.6 2.8 gather_fusion
  75.4 1.8 gather_fusion.2
  81.5 2.8 gather_fusion
  84.3 1.8 gather_fusion.2
  90.5 2.8 gather_fusion
  99.4 2.8 gather_fusion
  102.1 1.8 gather_fusion.2
  108.3 2.8 gather_fusion
  117.2 2.8 gather_fusion
  126.1 2.8 gather_fusion
  135.0 2.8 gather_fusion
  143.9 2.8 gather_fusion
  152.8 2.8 gather_fusion
  161.7 2.8 gather_fusion
  170.6 2.8 gather_fusion
  177.0 27.6 %reduce-scatter.2.cloned.1.call-done = f32[128,256]{1,0:T(8,128)} async-done(((f32[256,256]{1,0:T(8,128)}), f32[128,256]{1,0:T(8,128)}) %reduce-scatter.2.cloned.1.call-update) | async-done | bytes 131088 | tf_op jit(solution)/shard_map/reduce_scatter | solution.py:44
  204.5 1.8 convolution_bitcast_fusion
  208.1 128.4 %all-reduce.2.cloned.1.call-done = f32[256,256]{0,1:T(8,128)} async-done(((f32[256,256]{0,1:T(8,128)}), f32[256,256]{0,1:T(8,128)}) %all-reduce.2.cloned.1.call-update) | async-done | bytes 262160 | tf_op jit(solution)/shard_map/psum | solution.py:52
  (151 shorter events, 81.9 us)
Async XLA Ops:
  7.2 199.2 %copy-start = (bf16[256,256]{1,0:T(8,128)(2,1)S(1)}, bf16[256,256]{1,0:T(8,128)(2,1)}, u32[]{:S(2)}) copy-start(bf16[256,256]{1,0:T(8,128)(2,1)} %param.13) | copy-start | bytes 393220
  7.2 44.2 %all-gather.2.cloned.1.call-start = ((), (), s32[]{:S(2)}) async-start(), calls=%async_computation.1 | async-start | bytes 1114112 | tf_op jit(solution)/shard_map/all_gather | solution.py:39
  8.9 195.7 %reduce-scatter.2.cloned.1.call-start = ((), (), s32[]{:S(2)}) async-start(), calls=%async_computation.2 | async-start | bytes 393216 | tf_op jit(solution)/shard_map/reduce_scatter | solution.py:44
  51.5 153.0 %copy-start.1 = (bf16[128,256]{1,0:T(8,128)(2,1)S(1)}, bf16[128,256]{1,0:T(8,128)(2,1)}, u32[]{:S(2)}) copy-start(bf16[128,256]{1,0:T(8,128)(2,1)} %param.12) | copy-start | bytes 196612
  176.9 159.6 %all-reduce.2.cloned.1.call-start = ((), (), s32[]{:S(2)}) async-start(), calls=%async_computation.3 | async-start | bytes 524288 | tf_op jit(solution)/shard_map/psum | solution.py:52
Sparse Core Ops, SparseCore 0:
  10.7 40.6 all-gather.1
  177.0 27.4 reduce-scatter.1
  211.5 124.9 all-reduce.1
where the time goes:
time: 347 us; the launch traced here: 345 us
  waiting for transfers between devices  198 us (57%)
  local copies, waits for them, and re-layouts  102 us (29%)
  matrix products  17.1 us (5%)
  between operations  14.4 us (4%)
  other arithmetic  12.1 us (3%)
    psum x1, waiting for transfers between devices, body(): lax.psum(local_terms, ('rep', 'row')) * (1.0 / nodes_total ** 0.5)  128 us
    gather x28, local copies, waits for them, and re-layouts, one_turn(): picked = sources[cols_ids[clipped]]  43.5 us
    all_gather x1, waiting for transfers between devices, body(): group_rows = lax.all_gather(masked, 'row', axis=0, tiled=True)  41.8 us
    gather x14, local copies, waits for them, and re-layouts, one_turn(): tile_block = values[clipped]  39 us
    reduce_scatter x1, waiting for transfers between devices, body(): lax.psum_scatter(partial_value, 'rep', scatter_dimension=0, tiled=True)  27.6 us
    gather x14, local copies, waits for them, and re-layouts, one_turn(): rows_ids[clipped][None, :]  18.2 us
    dot_general x14, matrix products, one_turn(): jnp.einsum('rk,kaf->raf', onehot.astype(jnp.float32), products)  9.56 us
    lt x14, other arithmetic, one_turn(): alive_mask = slot_ids < live_count  9.14 us
  transfers between devices with their start and end apart: 3, of which 3 were waited for; matrix products, arithmetic and copies ran while one was open for 1% of the time, Pallas kernels for 0%

commit v1 on v0

--- a/solution.py
+++ b/solution.py
@@ -1,9 +1,14 @@
+import functools
+
 import jax
 import jax.numpy as jnp
 from jax import lax
+from jax.experimental import pallas as pl
+from jax.experimental.pallas import tpu as pltpu
 from jax.sharding import PartitionSpec as P
 
 slot_group = 8
+both = ("rep", "row")
 
 
 def tile_pass(values, rows_ids, cols_ids, live_count, sources, out_blocks):
@@ -30,7 +35,7 @@
     return lax.fori_loop(0, turn_count, one_turn, start_totals)
 
 
-def body(grad_out, relu_mask, layer_input, weight, tile_values, tile_rows, tile_cols, tile_count):
+def general_body(grad_out, relu_mask, layer_input, weight, tile_values, tile_rows, tile_cols, tile_count):
     block_rows = tile_values.shape[1]
     features = grad_out.shape[1]
     out_blocks = lax.axis_size("rep")
@@ -49,21 +54,172 @@
     local_terms = lax.dot_general(
         layer_input, prop_rounded, (((0,), (0,)), ((), ())), preferred_element_type=jnp.float32
     )
-    grad_weight = lax.psum(local_terms, ("rep", "row")) * (1.0 / nodes_total**0.5)
+    grad_weight = lax.psum(local_terms, both) * (1.0 / nodes_total**0.5)
+    return (grad_input, grad_weight)
+
+
+def swap(value, mask, total):
+    return lax.ppermute(value, both, [(i, i ^ mask) for i in range(total)])
+
+
+def merge_kernel(order, group, place_ref, rows_ref, cols_ref, count_ref, values_ref, out_ref, staged, sums, sems):
+    slots = values_ref.shape[0]
+    sources = len(order)
+    blk = values_ref.shape[1]
+    count = count_ref[0]
+    pieces = slots // group
+
+    def piece_copy(i):
+        part = pl.ds(i * group, group)
+        return pltpu.make_async_copy(values_ref.at[part], staged.at[part], sems.at[i])
+
+    for i in range(pieces):
+        @pl.when(i * group < count)
+        def _(i=i):
+            piece_copy(i).start()
+
+    sums[...] = jnp.zeros_like(sums)
+    rep_id = place_ref[0]
+    row_id = place_ref[1]
+    for i in range(pieces):
+        @pl.when(i * group < count)
+        def _(i=i):
+            piece_copy(i).wait()
+
+            def add_one(k, carry):
+                spot = (rows_ref[k] ^ rep_id) * sources + (cols_ref[k] ^ row_id)
+                sums[spot] += staged[k].astype(jnp.float32)
+                return carry
+
+            lax.fori_loop(i * group, jnp.minimum(count, (i + 1) * group), add_one, 0)
+
+    for r in range(out_ref.shape[0] // blk):
+        for at, offset in enumerate(order):
+            out_ref[r * blk:(r + 1) * blk, at * blk:(at + 1) * blk] = sums[r * sources + offset].astype(out_ref.dtype)
+
+
+def merge_tiles(place, rows, cols, count, values, order, out_blocks):
+    slots, blk, _ = values.shape
+    group = 16
+    smem = pl.BlockSpec(memory_space=pltpu.SMEM)
+    return pl.pallas_call(
+        functools.partial(merge_kernel, order, group),
+        out_shape=jax.ShapeDtypeStruct((out_blocks * blk, len(order) * blk), jnp.bfloat16),
+        in_specs=[smem, smem, smem, smem, pl.BlockSpec(memory_space=pl.ANY)],
+        out_specs=pl.BlockSpec(memory_space=pltpu.VMEM),
+        scratch_shapes=[
+            pltpu.VMEM(values.shape, values.dtype),
+            pltpu.VMEM((out_blocks * len(order), blk, blk), jnp.float32),
+            pltpu.SemaphoreType.DMA((slots // group,)),
+        ],
+        compiler_params=pltpu.CompilerParams(vmem_limit_bytes=24 * 1024 * 1024),
+        cost_estimate=pl.CostEstimate(flops=slots * blk * blk, bytes_accessed=4 * slots * blk * blk, transcendentals=0),
+    )(place, rows, cols, count, values)
+
+
+def product_kernel(scale, place_ref, tiles_ref, near_ref, far_ref, own_in_ref, peer_in_ref, keep_ref, send_ref, own_ref, peer_ref):
+    half = near_ref.shape[0]
+    blk = own_in_ref.shape[0]
+    total = jnp.dot(tiles_ref[:, :half], near_ref[...], preferred_element_type=jnp.float32)
+    total += jnp.dot(tiles_ref[:, half:], far_ref[...], preferred_element_type=jnp.float32)
+    own_ref[...] = total[:blk]
+    peer_ref[...] = total[blk:].astype(peer_ref.dtype)
+    rounded = total.astype(jnp.bfloat16)
+    across = (((0,), (0,)), ((), ()))
+    terms = lax.dot_general(own_in_ref[...], rounded[:blk], across, preferred_element_type=jnp.float32)
+    terms += lax.dot_general(peer_in_ref[...], rounded[blk:], across, preferred_element_type=jnp.float32)
+    terms *= scale
+    rows = terms.shape[0] // 2
+    upper = place_ref[2] == 0
+    keep_ref[...] = jnp.where(upper, terms[:rows], terms[rows:])
+    send_ref[...] = jnp.where(upper, terms[rows:], terms[:rows])
+
+
+def products(place, tiles, near, far, own_in, peer_in, scale):
+    blk, features = own_in.shape
+    vmem = pl.BlockSpec(memory_space=pltpu.VMEM)
+    part = (own_in.shape[1] // 2, features)
+    return pl.pallas_call(
+        functools.partial(product_kernel, scale),
+        out_shape=[
+            jax.ShapeDtypeStruct(part, jnp.float32),
+            jax.ShapeDtypeStruct(part, jnp.float32),
+            jax.ShapeDtypeStruct((blk, features), jnp.float32),
+            jax.ShapeDtypeStruct((blk, features), jnp.bfloat16),
+        ],
+        in_specs=[pl.BlockSpec(memory_space=pltpu.SMEM)] + [vmem] * 5,
+        out_specs=[vmem] * 4,
+        compiler_params=pltpu.CompilerParams(vmem_limit_bytes=24 * 1024 * 1024),
+        cost_estimate=pl.CostEstimate(flops=2 * tiles.size * features, bytes_accessed=4 * tiles.size, transcendentals=0),
+    )(place, tiles, near, far, own_in, peer_in)
+
+
+def quad_sum(value, low, high, total):
+    first = swap(value, low, total)
+    second = swap(value, high, total)
+    third = swap(value, low | high, total)
+    f32 = jnp.float32
+    return (value.astype(f32) + first.astype(f32)) + (second.astype(f32) + third.astype(f32))
+
+
+def pair_body(grad_out, relu_mask, layer_input, weight, tile_values, tile_rows, tile_cols, tile_count):
+    rep, row = lax.axis_size("rep"), lax.axis_size("row")
+    total = rep * row
+    blk = tile_values.shape[1]
+    masked = grad_out * relu_mask.astype(jnp.bfloat16)
+    rep_id, row_id = lax.axis_index("rep"), lax.axis_index("row")
+    core_id = row_id % 2
+    place = jnp.stack([rep_id, row_id, core_id]).astype(jnp.int32)
+
+    order = [0]
+    gathered = [masked]
+    top = row // 4
+    gathered = [masked] + [swap(masked, m, total) for m in (top, 2 * top, 3 * top)]
+    order = [0, top, 2 * top, 3 * top]
+    near = jnp.concatenate(gathered, 0)
+    bit = top // 2
+    while bit > 1:
+        near = jnp.concatenate([near, swap(near, bit, total)], 0)
+        order = order + [o ^ bit for o in order]
+        bit //= 2
+    far = swap(near, 1, total)
+    order = order + [o ^ 1 for o in order]
+    peer_in = swap(layer_input, row, total)
+    tiles = merge_tiles(place, tile_rows, tile_cols, tile_count, tile_values, order, rep)
+    keep, send, own, peer = products(place, tiles, near, far, layer_input, peer_in, 1.0 / (blk * total) ** 0.5)
+
+    part = (keep + swap(send, 1, total)).astype(jnp.bfloat16)
+    part = lax.optimization_barrier(part)
+    part = quad_sum(part, row, top // 2, total).astype(jnp.bfloat16)
+    part = lax.optimization_barrier(part)
+    part = quad_sum(part, top, 2 * top, total)
+    part = lax.optimization_barrier(part)
+    other = swap(part, 1, total)
+    grad_weight = jnp.where(core_id == 0, jnp.concatenate([part, other], 0), jnp.concatenate([other, part], 0))
+
+    prop = (own + swap(peer, row, total).astype(jnp.float32)).astype(jnp.bfloat16)
+    grad_input = lax.dot_general(
+        prop, weight, (((1,), (1,)), ((), ())), preferred_element_type=jnp.float32
+    ).astype(jnp.bfloat16)
     return (grad_input, grad_weight)
 
 
 def solution(mesh):
     placed = (
-        P(("rep", "row"), None),
-        P(("rep", "row"), None),
-        P(("rep", "row"), None),
+        P(both, None),
+        P(both, None),
+        P(both, None),
         P(),
-        P(("rep", "row"), None, None),
-        P(("rep", "row")),
-        P(("rep", "row")),
-        P(("rep", "row")),
+        P(both, None, None),
+        P(both),
+        P(both),
+        P(both),
     )
+    merged = mesh.shape["rep"] == 2 and mesh.shape["row"] == 16
     return jax.shard_map(
-        body, mesh=mesh, in_specs=placed, out_specs=(P(("rep", "row"), None), P()), check_vma=False
+        pair_body if merged else general_body,
+        mesh=mesh,
+        in_specs=placed,
+        out_specs=(P(both, None), P()),
+        check_vma=False,
     )

time: 347 us -> 49 us (0.14)
  waiting for transfers between devices: 198 us -> 18.9 us
  local copies, waits for them, and re-layouts: 102 us -> 3.55 us
  starting transfers between devices: 0.12 us -> 18.6 us
  matrix products: 17.1 us -> 0.83 us
  between operations: 14.4 us -> 1.42 us
  other arithmetic: 12.1 us -> 1.91 us
  Pallas kernels: 0 us -> 3.73 us
    psum x1 -> x0, waiting for transfers between devices: 128 us -> none  [body(): lax.psum(local_terms, ('rep', 'row')) * (1.0 / nodes_total ** 0.5)]
    gather x56 -> x0, local copies, waits for them, and re-layouts: 101 us -> none  [the longest x28 43.5 us: one_turn(): picked = sources[cols_ids[clipped]]]
    all_gather x1 -> x0, waiting for transfers between devices: 41.8 us -> none  [body(): group_rows = lax.all_gather(masked, 'row', axis=0, tiled=True)]
    reduce_scatter x1 -> x0, waiting for transfers between devices: 27.6 us -> none  [body(): lax.psum_scatter(partial_value, 'rep', scatter_dimension=0, tiled=True)]
    ppermute x0 -> x15, waiting for transfers between devices: none -> 18.9 us  [swap(): return lax.ppermute(value, both, [(i, i ^ mask) for i in range(total)])]
    ppermute x0 -> x15, starting transfers between devices: none -> 18.6 us  [swap(): return lax.ppermute(value, both, [(i, i ^ mask) for i in range(total)])]
    dot_general x30 -> x1, matrix products: 17.1 us -> 0.83 us  [pair_body(): lax.dot_general(prop, weight, (((1,), (1,)), ((), ())), preferred_element...]
    lt x14 -> x0, other arithmetic: 9.14 us -> none  [one_turn(): alive_mask = slot_ids < live_count]
  transfers between devices with their start and end apart: 3 -> 15, of which waited for: 3 -> 9; matrix products, arithmetic and copies ran while one was open for 1% -> 2% of each run, Pallas kernels for 0% -> 5%
where the time goes in v1:
time: 49 us
  waiting for transfers between devices  18.9 us (39%)
  starting transfers between devices  18.6 us (38%)
  Pallas kernels  3.73 us (8%)
  local copies, waits for them, and re-layouts  3.55 us (7%)
  other arithmetic  1.91 us (4%)
  between operations  1.42 us (3%)
  matrix products  0.83 us (2%)
    ppermute x15, waiting for transfers between devices, swap(): return lax.ppermute(value, both, [(i, i ^ mask) for i in range(total)])  18.9 us
    ppermute x15, starting transfers between devices, swap(): return lax.ppermute(value, both, [(i, i ^ mask) for i in range(total)])  18.6 us
    unnamed x13, local copies, waits for them, and re-layouts  3.53 us
    pallas_call x1, Pallas kernels, merge_tiles(): pl.pallas_call(functools.partial(merge_kernel, order, group), out_shape=j...  2.42 us
    pallas_call x1, Pallas kernels, products(): pl.pallas_call(functools.partial(product_kernel, scale), out_shape=[jax.S...  1.31 us
    unnamed x1, other arithmetic  1.01 us
  transfers between devices with their start and end apart: 15, of which 9 were waited for; matrix products, arithmetic and copies ran while one was open for 2% of the time, Pallas kernels for 5%

profile of v1, /device:TPU:0, one launch (start us, length us, event | category | flops | bytes accessed | tf_op | source)
XLA Modules:
  0.0 49.0 jit_solution(9638447502555803039)
XLA Ops:
  0.7 1.0 %constant_dynamic-update-slice_fusion.4 = (bf16[1024,256]{1,0:T(8,128)(2,1)S(1)}, bf16[128,256]{1,0:T(8,128)(2,1)S(1)}) fusion(bf16[128,256]{1,0:T(8,128)(2,1)} %param.8, s32[128,256]{1,0:T(8,128)} %param.9), kind=kLoop, calls=%fused_computation.12 | loop fusion | flops 163839 | bytes 327680
  1.7 5.1 %collective-permute-start.2 = (bf16[128,256]{1,0:T(8,128)(2,1)S(1)}, bf16[128,256]{1,0:T(8,128)(2,1)S(1)}, u32[]{:S(2)}, u32[]{:S(2)}) collective-permute-start(bf16[128,256]{1,0:T(8,128)(2,1)S(1)} %get-tuple-element.11), channel_id=1, source_target_pairs={{0,12},{1,13},{2,14},{3,15},{4,8},{5,9},{6,10},{7,11},{8,4},{9,5},... | collective-permute-start | bytes 196616 | tf_op jit(solution)/shard_map/ppermute | solution.py:62
  7.4 1.9 %collective-permute-done.2 = bf16[128,256]{1,0:T(8,128)(2,1)S(1)} collective-permute-done((bf16[128,256]{1,0:T(8,128)(2,1)S(1)}, bf16[128,256]{1,0:T(8,128)(2,1)S(1)}, u32[]{:S(2)}, u32[]{:S(2)}) %collective-permute-start.2) | collective-permute-done | bytes 65568 | tf_op jit(solution)/shard_map/ppermute | solution.py:62
  9.4 3.0 %collective-permute-done.1 = bf16[128,256]{1,0:T(8,128)(2,1)S(1)} collective-permute-done((bf16[128,256]{1,0:T(8,128)(2,1)S(1)}, bf16[128,256]{1,0:T(8,128)(2,1)S(1)}, u32[]{:S(2)}, u32[]{:S(2)}) %collective-permute-start.1) | collective-permute-done | bytes 65568 | tf_op jit(solution)/shard_map/ppermute | solution.py:62
  12.4 1.6 %collective-permute-start.3 = (bf16[512,256]{1,0:T(8,128)(2,1)S(1)}, bf16[512,256]{1,0:T(8,128)(2,1)S(1)}, u32[]{:S(2)}, u32[]{:S(2)}) collective-permute-start(bf16[512,256]{1,0:T(8,128)(2,1)S(1)} %pad_maximum_fusion), channel_id=1, source_target_pairs={{0,2},{1,3},{2,0},{3,1},{4,6},{5,7},{6,4},{7,5},{8,10},{9,11},{10,... | collective-permute-start | bytes 786440 | tf_op jit(solution)/shard_map/ppermute | solution.py:62
  14.0 6.3 %collective-permute-done.3 = bf16[512,256]{1,0:T(8,128)(2,1)S(1)} collective-permute-done((bf16[512,256]{1,0:T(8,128)(2,1)S(1)}, bf16[512,256]{1,0:T(8,128)(2,1)S(1)}, u32[]{:S(2)}, u32[]{:S(2)}) %collective-permute-start.3) | collective-permute-done | bytes 262176 | tf_op jit(solution)/shard_map/ppermute | solution.py:62
  20.5 1.7 %collective-permute-start.5 = (bf16[128,256]{1,0:T(8,128)(2,1)}, bf16[128,256]{1,0:T(8,128)(2,1)S(1)}, u32[]{:S(2)}, u32[]{:S(2)}) collective-permute-start(bf16[128,256]{1,0:T(8,128)(2,1)} %own_in_ref.1), channel_id=1, source_target_pairs={{0,16},{1,17},{2,18},{3,19},{4,20},{5,21},{6,22},{7,23},{8,24},{9,... | collective-permute-start | bytes 196616 | tf_op jit(solution)/shard_map/ppermute | solution.py:62
  22.9 2.2 %copy-done.1 = bf16[128,128,128]{2,1,0:T(8,128)(2,1)S(1)} copy-done((bf16[128,128,128]{2,1,0:T(8,128)(2,1)S(1)}, bf16[128,128,128]{2,1,0:T(8,128)(2,1)}, u32[]{:S(2)}) %copy-start.1) | copy-done | bytes 4194328
  25.1 0.7 %copy-done.3 = s32[128]{0:T(128)S(1)} copy-done((s32[128]{0:T(128)S(1)}, s32[128]{0:T(128)}, u32[]{:S(2)}) %copy-start.3) | copy-done | bytes 536
  25.8 0.7 %copy-done.4 = s32[128]{0:T(128)S(1)} copy-done((s32[128]{0:T(128)S(1)}, s32[128]{0:T(128)}, u32[]{:S(2)}) %copy-start.4) | copy-done | bytes 536
  26.4 2.4 %shard_map.95.tiles_ref = bf16[256,2048]{1,0:T(8,128)(2,1)S(1)} custom-call(s32[3]{0:T(128)S(1)} %pad_add_fusion.place_ref, s32[128]{0:T(128)S(1)} %copy-done.3, s32[128]{0:T(128)S(1)} %copy-done.4, s32[1]{0:T(128)S(6)} %copy.14.count_ref, bf16[128,128,128]{2,1,0:T(8,128)(2,1)S(1)} %copy-done.1), custom_call_target="tpu_custom_call" | custom-call | flops 2097152 | bytes 8388608 | tf_op jit(solution)/shard_map/pallas_call | solution.py:105
  28.9 1.3 %shard_map.96 = (f32[128,256]{1,0:T(8,128)S(1)}, f32[128,256]{1,0:T(8,128)S(1)}, f32[128,256]{1,0:T(8,128)S(1)}, bf16[128,256]{1,0:T(8,128)(2,1)S(1)}) custom-call(s32[3]{0:T(128)S(1)} %pad_add_fusion.place_ref, bf16[256,2048]{1,0:T(8,128)(2,1)S(1)} %shard_map.95.tiles_ref, bf16[1024,256]{1,0:T(8,128)(2,1)S(1)} %constant_dynamic-update-slice_fusion.near_ref, ...), custom_call_target="tpu_custom_call" | custom-call | flops 268435456 | bytes 2097152 | tf_op jit(solution)/shard_map/pallas_call | solution.py:142
  30.3 1.3 %collective-permute-done.7 = f32[128,256]{1,0:T(8,128)S(1)} collective-permute-done((f32[128,256]{1,0:T(8,128)S(1)}, f32[128,256]{1,0:T(8,128)S(1)}, u32[]{:S(2)}, u32[]{:S(2)}) %collective-permute-start.7) | collective-permute-done | bytes 131104 | tf_op jit(solution)/shard_map/ppermute | solution.py:62
  31.6 1.5 %collective-permute-start.10 = (bf16[128,256]{1,0:T(8,128)(2,1)S(1)}, bf16[128,256]{1,0:T(8,128)(2,1)S(1)}, u32[]{:S(2)}, u32[]{:S(2)}) collective-permute-start(bf16[128,256]{1,0:T(8,128)(2,1)S(1)} %add_convert_fusion.1), channel_id=1, source_target_pairs={{0,18},{1,19},{2,16},{3,17},{4,22},{5,23},{6,20},{7,21},{8,26},{9,... | collective-permute-start | bytes 196616 | tf_op jit(solution)/shard_map/ppermute | solution.py:62
  33.1 2.0 %collective-permute-start.8 = (bf16[128,256]{1,0:T(8,128)(2,1)S(1)}, bf16[128,256]{1,0:T(8,128)(2,1)S(1)}, u32[]{:S(2)}, u32[]{:S(2)}) collective-permute-start(bf16[128,256]{1,0:T(8,128)(2,1)S(1)} %add_convert_fusion.1), channel_id=1, source_target_pairs={{0,16},{1,17},{2,18},{3,19},{4,20},{5,21},{6,22},{7,23},{8,24},{9,... | collective-permute-start | bytes 196616 | tf_op jit(solution)/shard_map/ppermute | solution.py:62
  35.2 1.7 %collective-permute-done.10 = bf16[128,256]{1,0:T(8,128)(2,1)S(1)} collective-permute-done((bf16[128,256]{1,0:T(8,128)(2,1)S(1)}, bf16[128,256]{1,0:T(8,128)(2,1)S(1)}, u32[]{:S(2)}, u32[]{:S(2)}) %collective-permute-start.10) | collective-permute-done | bytes 65568 | tf_op jit(solution)/shard_map/ppermute | solution.py:62
  36.9 1.2 %collective-permute-done.9 = bf16[128,256]{1,0:T(8,128)(2,1)S(1)} collective-permute-done((bf16[128,256]{1,0:T(8,128)(2,1)S(1)}, bf16[128,256]{1,0:T(8,128)(2,1)S(1)}, u32[]{:S(2)}, u32[]{:S(2)}) %collective-permute-start.9) | collective-permute-done | bytes 65568 | tf_op jit(solution)/shard_map/ppermute | solution.py:62
  38.2 1.9 %collective-permute-start.13 = (bf16[128,256]{1,0:T(8,128)(2,1)S(1)}, bf16[128,256]{1,0:T(8,128)(2,1)S(1)}, u32[]{:S(2)}, u32[]{:S(2)}) collective-permute-start(bf16[128,256]{1,0:T(8,128)(2,1)S(1)} %add_convert_fusion), channel_id=1, source_target_pairs={{0,12},{1,13},{2,14},{3,15},{4,8},{5,9},{6,10},{7,11},{8,4},{9,5},... | collective-permute-start | bytes 196616 | tf_op jit(solution)/shard_map/ppermute | solution.py:62
  40.1 2.6 %collective-permute-start.11 = (bf16[128,256]{1,0:T(8,128)(2,1)S(1)}, bf16[128,256]{1,0:T(8,128)(2,1)S(1)}, u32[]{:S(2)}, u32[]{:S(2)}) collective-permute-start(bf16[128,256]{1,0:T(8,128)(2,1)S(1)} %add_convert_fusion), channel_id=1, source_target_pairs={{0,4},{1,5},{2,6},{3,7},{4,0},{5,1},{6,2},{7,3},{8,12},{9,13},{10,... | collective-permute-start | bytes 196616 | tf_op jit(solution)/shard_map/ppermute | solution.py:62
  42.6 1.3 %collective-permute-start.6 = (bf16[128,256]{1,0:T(8,128)(2,1)S(1)}, bf16[128,256]{1,0:T(8,128)(2,1)S(1)}, u32[]{:S(2)}, u32[]{:S(2)}) collective-permute-start(bf16[128,256]{1,0:T(8,128)(2,1)S(1)} %get-tuple-element.7), channel_id=1, source_target_pairs={{0,16},{1,17},{2,18},{3,19},{4,20},{5,21},{6,22},{7,23},{8,24},{9,... | collective-permute-start | bytes 196616 | tf_op jit(solution)/shard_map/ppermute | solution.py:62
  43.9 1.1 %collective-permute-done.13 = bf16[128,256]{1,0:T(8,128)(2,1)S(1)} collective-permute-done((bf16[128,256]{1,0:T(8,128)(2,1)S(1)}, bf16[128,256]{1,0:T(8,128)(2,1)S(1)}, u32[]{:S(2)}, u32[]{:S(2)}) %collective-permute-start.13) | collective-permute-done | bytes 65568 | tf_op jit(solution)/shard_map/ppermute | solution.py:62
  45.1 1.7 %collective-permute-done.12 = bf16[128,256]{1,0:T(8,128)(2,1)S(1)} collective-permute-done((bf16[128,256]{1,0:T(8,128)(2,1)S(1)}, bf16[128,256]{1,0:T(8,128)(2,1)S(1)}, u32[]{:S(2)}, u32[]{:S(2)}) %collective-permute-start.12) | collective-permute-done | bytes 65568 | tf_op jit(solution)/shard_map/ppermute | solution.py:62
  46.9 0.8 %convolution_convert_fusion = bf16[128,256]{1,0:T(8,128)(2,1)} fusion(bf16[256,256]{1,0:T(8,128)(2,1)S(1)} %copy-done, f32[128,256]{1,0:T(8,128)S(1)} %get-tuple-element.6, bf16[128,256]{1,0:T(8,128)(2,1)S(1)} %collective-permute-done.6), kind=kOutput, calls=%fused_computation | convolution fusion | flops 16908288 | bytes 393216 | tf_op jit(solution)/shard_map/dot_general | solution.py:201
  48.3 0.7 %maximum_select_fusion = f32[256,256]{1,0:T(8,128)} fusion(f32[128,256]{1,0:T(8,128)S(1)} %collective-permute-done.14, f32[128,256]{1,0:T(8,128)S(1)} %add_add_fusion, pred[]{:T(512)S(6)} %eq.5), kind=kLoop, calls=%fused_computation.2 | loop fusion | flops 196608 | bytes 524289 | tf_op jit(solution)/shard_map/jit(_where)/select_n | solution.py:198
  (30 shorter events, 1.6 us)
Async XLA Ops:
  0.6 46.3 %copy-start = (bf16[256,256]{1,0:T(8,128)(2,1)S(1)}, bf16[256,256]{1,0:T(8,128)(2,1)}, u32[]{:S(2)}) copy-start(bf16[256,256]{1,0:T(8,128)(2,1)} %param.11) | copy-start | bytes 393220
  0.6 28.2 %copy-start.2 = (bf16[128,256]{1,0:T(8,128)(2,1)S(1)}, bf16[128,256]{1,0:T(8,128)(2,1)}, u32[]{:S(2)}) copy-start(bf16[128,256]{1,0:T(8,128)(2,1)} %own_in_ref.1) | copy-start | bytes 196612
  1.7 7.7 %collective-permute-start.2 = (bf16[128,256]{1,0:T(8,128)(2,1)S(1)}, bf16[128,256]{1,0:T(8,128)(2,1)S(1)}, u32[]{:S(2)}, u32[]{:S(2)}) collective-permute-start(bf16[128,256]{1,0:T(8,128)(2,1)S(1)} %get-tuple-element.11), channel_id=1, source_target_pairs={{0,12},{1,13},{2,14},{3,15},{4,8},{5,9},{6,10},{7,11},{8,4},{9,5},... | collective-permute-start | bytes 196616 | tf_op jit(solution)/shard_map/ppermute | solution.py:62
  6.8 5.6 %collective-permute-start.1 = (bf16[128,256]{1,0:T(8,128)(2,1)S(1)}, bf16[128,256]{1,0:T(8,128)(2,1)S(1)}, u32[]{:S(2)}, u32[]{:S(2)}) collective-permute-start(bf16[128,256]{1,0:T(8,128)(2,1)S(1)} %get-tuple-element.11), channel_id=1, source_target_pairs={{0,8},{1,9},{2,10},{3,11},{4,12},{5,13},{6,14},{7,15},{8,0},{9,1},... | collective-permute-start | bytes 196616 | tf_op jit(solution)/shard_map/ppermute | solution.py:62
  6.8 5.6 %collective-permute-start = (bf16[128,256]{1,0:T(8,128)(2,1)S(1)}, bf16[128,256]{1,0:T(8,128)(2,1)S(1)}, u32[]{:S(2)}, u32[]{:S(2)}) collective-permute-start(bf16[128,256]{1,0:T(8,128)(2,1)S(1)} %get-tuple-element.11), channel_id=1, source_target_pairs={{0,4},{1,5},{2,6},{3,7},{4,0},{5,1},{6,2},{7,3},{8,12},{9,13},{10,... | collective-permute-start | bytes 196616 | tf_op jit(solution)/shard_map/ppermute | solution.py:62
  12.4 7.9 %collective-permute-start.3 = (bf16[512,256]{1,0:T(8,128)(2,1)S(1)}, bf16[512,256]{1,0:T(8,128)(2,1)S(1)}, u32[]{:S(2)}, u32[]{:S(2)}) collective-permute-start(bf16[512,256]{1,0:T(8,128)(2,1)S(1)} %pad_maximum_fusion), channel_id=1, source_target_pairs={{0,2},{1,3},{2,0},{3,1},{4,6},{5,7},{6,4},{7,5},{8,10},{9,11},{10,... | collective-permute-start | bytes 786440 | tf_op jit(solution)/shard_map/ppermute | solution.py:62
  20.4 8.5 %collective-permute-start.4 = (bf16[1024,256]{1,0:T(8,128)(2,1)S(1)}, bf16[1024,256]{1,0:T(8,128)(2,1)S(1)}, u32[]{:S(2)}, u32[]{:S(2)}) collective-permute-start(bf16[1024,256]{1,0:T(8,128)(2,1)S(1)} %constant_dynamic-update-slice_fusion.near_ref), channel_id=1, source_target_pairs={{0,1},{1,0},{2,3},{3,2},{4,5},{5,4},{6,7},{7,6},{8,9},{9,8},{10,11... | collective-permute-start | bytes 1572872 | tf_op jit(solution)/shard_map/ppermute | solution.py:62
  20.5 8.4 %collective-permute-start.5 = (bf16[128,256]{1,0:T(8,128)(2,1)}, bf16[128,256]{1,0:T(8,128)(2,1)S(1)}, u32[]{:S(2)}, u32[]{:S(2)}) collective-permute-start(bf16[128,256]{1,0:T(8,128)(2,1)} %own_in_ref.1), channel_id=1, source_target_pairs={{0,16},{1,17},{2,18},{3,19},{4,20},{5,21},{6,22},{7,23},{8,24},{9,... | collective-permute-start | bytes 196616 | tf_op jit(solution)/shard_map/ppermute | solution.py:62
  22.9 2.2 %copy-start.1 = (bf16[128,128,128]{2,1,0:T(8,128)(2,1)S(1)}, bf16[128,128,128]{2,1,0:T(8,128)(2,1)}, u32[]{:S(2)}) copy-start(bf16[128,128,128]{2,1,0:T(8,128)(2,1)} %values_ref.1) | copy-start | bytes 12582916
  25.1 0.7 %copy-start.3 = (s32[128]{0:T(128)S(1)}, s32[128]{0:T(128)}, u32[]{:S(2)}) copy-start(s32[128]{0:T(128)} %rows_ref.1) | copy-start | bytes 1540
  25.8 0.7 %copy-start.4 = (s32[128]{0:T(128)S(1)}, s32[128]{0:T(128)}, u32[]{:S(2)}) copy-start(s32[128]{0:T(128)} %cols_ref.1) | copy-start | bytes 1540
  30.2 1.4 %collective-permute-start.7 = (f32[128,256]{1,0:T(8,128)S(1)}, f32[128,256]{1,0:T(8,128)S(1)}, u32[]{:S(2)}, u32[]{:S(2)}) collective-permute-start(f32[128,256]{1,0:T(8,128)S(1)} %get-tuple-element.9), channel_id=1, source_target_pairs={{0,1},{1,0},{2,3},{3,2},{4,5},{5,4},{6,7},{7,6},{8,9},{9,8},{10,11... | collective-permute-start | bytes 393224 | tf_op jit(solution)/shard_map/ppermute | solution.py:62
  31.6 5.3 %collective-permute-start.10 = (bf16[128,256]{1,0:T(8,128)(2,1)S(1)}, bf16[128,256]{1,0:T(8,128)(2,1)S(1)}, u32[]{:S(2)}, u32[]{:S(2)}) collective-permute-start(bf16[128,256]{1,0:T(8,128)(2,1)S(1)} %add_convert_fusion.1), channel_id=1, source_target_pairs={{0,18},{1,19},{2,16},{3,17},{4,22},{5,23},{6,20},{7,21},{8,26},{9,... | collective-permute-start | bytes 196616 | tf_op jit(solution)/shard_map/ppermute | solution.py:62
  33.1 5.0 %collective-permute-start.9 = (bf16[128,256]{1,0:T(8,128)(2,1)S(1)}, bf16[128,256]{1,0:T(8,128)(2,1)S(1)}, u32[]{:S(2)}, u32[]{:S(2)}) collective-permute-start(bf16[128,256]{1,0:T(8,128)(2,1)S(1)} %add_convert_fusion.1), channel_id=1, source_target_pairs={{0,2},{1,3},{2,0},{3,1},{4,6},{5,7},{6,4},{7,5},{8,10},{9,11},{10,... | collective-permute-start | bytes 196616 | tf_op jit(solution)/shard_map/ppermute | solution.py:62
  33.1 5.0 %collective-permute-start.8 = (bf16[128,256]{1,0:T(8,128)(2,1)S(1)}, bf16[128,256]{1,0:T(8,128)(2,1)S(1)}, u32[]{:S(2)}, u32[]{:S(2)}) collective-permute-start(bf16[128,256]{1,0:T(8,128)(2,1)S(1)} %add_convert_fusion.1), channel_id=1, source_target_pairs={{0,16},{1,17},{2,18},{3,19},{4,20},{5,21},{6,22},{7,23},{8,24},{9,... | collective-permute-start | bytes 196616 | tf_op jit(solution)/shard_map/ppermute | solution.py:62
  38.2 6.9 %collective-permute-start.13 = (bf16[128,256]{1,0:T(8,128)(2,1)S(1)}, bf16[128,256]{1,0:T(8,128)(2,1)S(1)}, u32[]{:S(2)}, u32[]{:S(2)}) collective-permute-start(bf16[128,256]{1,0:T(8,128)(2,1)S(1)} %add_convert_fusion), channel_id=1, source_target_pairs={{0,12},{1,13},{2,14},{3,15},{4,8},{5,9},{6,10},{7,11},{8,4},{9,5},... | collective-permute-start | bytes 196616 | tf_op jit(solution)/shard_map/ppermute | solution.py:62
  40.1 6.8 %collective-permute-start.12 = (bf16[128,256]{1,0:T(8,128)(2,1)S(1)}, bf16[128,256]{1,0:T(8,128)(2,1)S(1)}, u32[]{:S(2)}, u32[]{:S(2)}) collective-permute-start(bf16[128,256]{1,0:T(8,128)(2,1)S(1)} %add_convert_fusion), channel_id=1, source_target_pairs={{0,8},{1,9},{2,10},{3,11},{4,12},{5,13},{6,14},{7,15},{8,0},{9,1},... | collective-permute-start | bytes 196616 | tf_op jit(solution)/shard_map/ppermute | solution.py:62
  40.1 6.8 %collective-permute-start.11 = (bf16[128,256]{1,0:T(8,128)(2,1)S(1)}, bf16[128,256]{1,0:T(8,128)(2,1)S(1)}, u32[]{:S(2)}, u32[]{:S(2)}) collective-permute-start(bf16[128,256]{1,0:T(8,128)(2,1)S(1)} %add_convert_fusion), channel_id=1, source_target_pairs={{0,4},{1,5},{2,6},{3,7},{4,0},{5,1},{6,2},{7,3},{8,12},{9,13},{10,... | collective-permute-start | bytes 196616 | tf_op jit(solution)/shard_map/ppermute | solution.py:62
  42.6 4.3 %collective-permute-start.6 = (bf16[128,256]{1,0:T(8,128)(2,1)S(1)}, bf16[128,256]{1,0:T(8,128)(2,1)S(1)}, u32[]{:S(2)}, u32[]{:S(2)}) collective-permute-start(bf16[128,256]{1,0:T(8,128)(2,1)S(1)} %get-tuple-element.7), channel_id=1, source_target_pairs={{0,16},{1,17},{2,18},{3,19},{4,20},{5,21},{6,22},{7,23},{8,24},{9,... | collective-permute-start | bytes 196616 | tf_op jit(solution)/shard_map/ppermute | solution.py:62
  46.8 1.4 %collective-permute-start.14 = (f32[128,256]{1,0:T(8,128)S(1)}, f32[128,256]{1,0:T(8,128)S(1)}, u32[]{:S(2)}, u32[]{:S(2)}) collective-permute-start(f32[128,256]{1,0:T(8,128)S(1)} %add_add_fusion), channel_id=1, source_target_pairs={{0,1},{1,0},{2,3},{3,2},{4,5},{5,4},{6,7},{7,6},{8,9},{9,8},{10,11... | collective-permute-start | bytes 393224 | tf_op jit(solution)/shard_map/ppermute | solution.py:62

commit v2 on v1

v2 whole, which is shorter than its diff:
```python
import functools

import jax
import jax.numpy as jnp
from jax import lax
from jax.experimental import pallas as pl
from jax.experimental.pallas import tpu as pltpu
from jax.sharding import PartitionSpec as P

slot_group = 8
both = ("rep", "row")


def tile_pass(values, rows_ids, cols_ids, live_count, sources, out_blocks):
    block_rows = values.shape[1]
    features = sources.shape[2]
    slot_total = values.shape[0]

    def one_turn(turn_id, totals):
        slot_ids = turn_id * slot_group + jnp.arange(slot_group, dtype=jnp.int32)
        alive_mask = slot_ids < live_count
        clipped = jnp.minimum(slot_ids, slot_total - 1)
        tile_block = values[clipped]
        picked = sources[cols_ids[clipped]]
        products = jnp.einsum(
            "kab,kbf->kaf", tile_block, picked, preferred_element_type=jnp.float32
        )
        onehot = (
            rows_ids[clipped][None, :] == jnp.arange(out_blocks, dtype=jnp.int32)[:, None]
        ) & alive_mask[None, :]
        return totals + jnp.einsum("rk,kaf->raf", onehot.astype(jnp.float32), products)

    turn_count = (live_count + slot_group - 1) // slot_group
    start_totals = jnp.zeros((out_blocks, block_rows, features), jnp.float32)
    return lax.fori_loop(0, turn_count, one_turn, start_totals)


def general_body(grad_out, relu_mask, layer_input, weight, tile_values, tile_rows, tile_cols, tile_count):
    block_rows = tile_values.shape[1]
    features = grad_out.shape[1]
    out_blocks = lax.axis_size("rep")
    nodes_total = block_rows * lax.axis_size("rep") * lax.axis_size("row")
    masked = grad_out * relu_mask.astype(jnp.bfloat16)
    group_rows = lax.all_gather(masked, "row", axis=0, tiled=True)
    sources = group_rows.reshape(-1, block_rows, features)
    live_count = tile_count[0]
    partial_value = tile_pass(tile_values, tile_rows, tile_cols, live_count, sources, out_blocks)
    partial_value = partial_value.reshape(out_blocks * block_rows, features)
    owned = lax.psum_scatter(partial_value, "rep", scatter_dimension=0, tiled=True)
    prop_rounded = owned.astype(jnp.bfloat16)
    grad_input = lax.dot_general(
        prop_rounded, weight, (((1,), (1,)), ((), ())), preferred_element_type=jnp.float32
    ).astype(jnp.bfloat16)
    local_terms = lax.dot_general(
        layer_input, prop_rounded, (((0,), (0,)), ((), ())), preferred_element_type=jnp.float32
    )
    grad_weight = lax.psum(local_terms, both) * (1.0 / nodes_total**0.5)
    return (grad_input, grad_weight)


def swap(value, mask, total):
    return lax.ppermute(value, both, [(i, i ^ mask) for i in range(total)])


def merge_kernel(order, group, spots_ref, values_ref, *rest):
    halves, (staged, sems), sums = rest[:2], rest[2:4], rest[4:]
    slots = values_ref.shape[0]
    sources = len(order)
    blk = values_ref.shape[1]
    count = spots_ref[slots]
    pieces = slots // group
    ways = len(sums)
    spare = sums[0].shape[0] - 1

    def piece_copy(i):
        part = pl.ds(i * group, group)
        return pltpu.make_async_copy(values_ref.at[part], staged.at[part], sems.at[i])

    for i in range(pieces):
        @pl.when(i * group < count)
        def _(i=i):
            piece_copy(i).start()

    for total in sums:
        total[...] = jnp.zeros_like(total)
    for i in range(pieces):
        @pl.when(i * group < count)
        def _(i=i):
            piece_copy(i).wait()

            def add_some(turn, carry):
                for way, total in enumerate(sums):
                    k = turn * ways + way
                    spot = jnp.where(k < count, spots_ref[k], spare)
                    total[spot] += staged[k].astype(jnp.float32)
                return carry

            last = jnp.minimum(count, (i + 1) * group)
            lax.fori_loop(i * group // ways, (last + ways - 1) // ways, add_some, 0)

    for h, half in enumerate(halves):
        across = half.shape[1] // blk
        for r in range(half.shape[0] // blk):
            for at in range(across):
                spot = r * sources + order[h * across + at]
                half[r * blk:(r + 1) * blk, at * blk:(at + 1) * blk] = sum(total[spot] for total in sums).astype(half.dtype)


def merge_tiles(spots, values, order, out_blocks):
    slots, blk, _ = values.shape
    group, ways = 16, 2
    smem = pl.BlockSpec(memory_space=pltpu.SMEM)
    vmem = pl.BlockSpec(memory_space=pltpu.VMEM)
    half = jax.ShapeDtypeStruct((out_blocks * blk, len(order) // 2 * blk), jnp.bfloat16)
    return pl.pallas_call(
        functools.partial(merge_kernel, order, group),
        out_shape=[half, half],
        in_specs=[smem, pl.BlockSpec(memory_space=pltpu.HBM)],
        out_specs=[vmem, vmem],
        scratch_shapes=[
            pltpu.VMEM(values.shape, values.dtype),
            pltpu.SemaphoreType.DMA((slots // group,)),
        ] + [pltpu.VMEM((out_blocks * len(order) + 1, blk, blk), jnp.float32)] * ways,
        compiler_params=pltpu.CompilerParams(vmem_limit_bytes=50 * 1024 * 1024),
        cost_estimate=pl.CostEstimate(flops=slots * blk * blk, bytes_accessed=4 * slots * blk * blk, transcendentals=0),
    )(spots, values)


def product_kernel(scale, place_ref, own_tiles_ref, twin_tiles_ref, near_ref, own_in_ref, twin_in_ref, keep_ref, send_ref, own_ref, twin_ref):
    own = jnp.dot(own_tiles_ref[...], near_ref[...], preferred_element_type=jnp.float32)
    twin = jnp.dot(twin_tiles_ref[...], near_ref[...], preferred_element_type=jnp.float32)
    own_ref[...] = own
    twin_ref[...] = twin.astype(twin_ref.dtype)
    across = (((0,), (0,)), ((), ()))
    terms = lax.dot_general(own_in_ref[...], own.astype(jnp.bfloat16), across, preferred_element_type=jnp.float32)
    terms += lax.dot_general(twin_in_ref[...], twin.astype(jnp.bfloat16), across, preferred_element_type=jnp.float32)
    terms *= scale
    rows = terms.shape[0] // 2
    upper = place_ref[0] == 0
    keep_ref[...] = jnp.where(upper, terms[:rows], terms[rows:])
    send_ref[...] = jnp.where(upper, terms[rows:], terms[:rows])


def products(place, own_tiles, twin_tiles, near, own_in, twin_in, scale):
    rows, features = own_tiles.shape[0], near.shape[1]
    vmem = pl.BlockSpec(memory_space=pltpu.VMEM)
    part = (own_in.shape[1] // 2, features)
    return pl.pallas_call(
        functools.partial(product_kernel, scale),
        out_shape=[
            jax.ShapeDtypeStruct(part, jnp.float32),
            jax.ShapeDtypeStruct(part, jnp.float32),
            jax.ShapeDtypeStruct((rows, features), jnp.float32),
            jax.ShapeDtypeStruct((rows, features), jnp.bfloat16),
        ],
        in_specs=[pl.BlockSpec(memory_space=pltpu.SMEM)] + [vmem] * 5,
        out_specs=[vmem] * 4,
        compiler_params=pltpu.CompilerParams(vmem_limit_bytes=24 * 1024 * 1024),
        cost_estimate=pl.CostEstimate(flops=4 * own_tiles.size * features, bytes_accessed=4 * own_tiles.size, transcendentals=0),
    )(place, own_tiles, twin_tiles, near, own_in, twin_in)


def quad_sum(value, low, high, total):
    third = swap(value, low | high, total)
    second = swap(value, high, total)
    first = swap(value, low, total)
    f32 = jnp.float32
    return (third.astype(f32) + second.astype(f32)) + (first.astype(f32) + value.astype(f32))


def pair_body(grad_out, relu_mask, layer_input, weight, tile_values, tile_rows, tile_cols, tile_count):
    rep, row = lax.axis_size("rep"), lax.axis_size("row")
    total = rep * row
    blk = tile_values.shape[1]
    masked = grad_out * relu_mask.astype(jnp.bfloat16)
    rep_id, row_id = lax.axis_index("rep"), lax.axis_index("row")
    core_id = row_id % 2
    place = core_id.astype(jnp.int32).reshape(1)

    top = row // 4
    order = [0, 3 * top, 2 * top, top]
    near = jnp.concatenate([masked] + [swap(masked, m, total) for m in order[1:]], 0)
    spots = (tile_rows ^ rep_id) * row + (tile_cols ^ row_id)
    spots = jnp.concatenate([spots, tile_count])
    order = order + [o + 2 for o in order]
    order = order + [o + 1 for o in order]
    own_tiles, far_tiles = merge_tiles(spots, tile_values, order, rep)
    near, own_tiles, far_tiles, own_in = lax.optimization_barrier((near, own_tiles, far_tiles, layer_input))
    near = jnp.concatenate([near, swap(near, 2, total)], 0)
    own_in = jnp.concatenate([own_in, swap(own_in, row, total)], 0)
    twin_tiles = swap(far_tiles, 1, total)
    own_in, twin_tiles = lax.optimization_barrier((own_in, twin_tiles))
    twin_in = swap(own_in, 1, total)
    near, own_in, twin_in, twin_tiles = lax.optimization_barrier((near, own_in, twin_in, twin_tiles))
    keep, send, own, twin = products(place, own_tiles, twin_tiles, near, own_in, twin_in, 1.0 / (blk * total) ** 0.5)

    part = (keep + swap(send, 1, total)).astype(jnp.bfloat16)
    part = lax.optimization_barrier(part)
    part = quad_sum(part, row, top // 2, total).astype(jnp.bfloat16)
    part = lax.optimization_barrier(part)
    part = quad_sum(part, top, 2 * top, total)
    part = lax.optimization_barrier(part)
    other = swap(part, 1, total)
    grad_weight = jnp.where(core_id == 0, jnp.concatenate([part, other], 0), jnp.concatenate([other, part], 0))

    own = own + swap(twin, 1, total).astype(jnp.float32)
    peer = swap(own[blk:].astype(jnp.bfloat16), row, total)
    prop = (own[:blk] + peer.astype(jnp.float32)).astype(jnp.bfloat16)
    grad_input = lax.dot_general(
        prop, weight, (((1,), (1,)), ((), ())), preferred_element_type=jnp.float32
    ).astype(jnp.bfloat16)
    return (grad_input, grad_weight)


def solution(mesh):
    placed = (
        P(both, None),
        P(both, None),
        P(both, None),
        P(),
        P(both, None, None),
        P(both),
        P(both),
        P(both),
    )
    merged = mesh.shape["rep"] == 2 and mesh.shape["row"] == 16
    return jax.shard_map(
        pair_body if merged else general_body,
        mesh=mesh,
        in_specs=placed,
        out_specs=(P(both, None), P()),
        check_vma=False,
    )
```

time: 49 us -> 41.5 us (0.85)
  local copies, waits for them, and re-layouts: 3.55 us -> 0.02 us
  waiting for transfers between devices: 18.9 us -> 15.6 us
  Pallas kernels: 3.73 us -> 3.05 us
  other arithmetic: 1.91 us -> 2.59 us
  starting transfers between devices: 18.6 us -> 18 us
    unnamed x13 -> x4, local copies, waits for them, and re-layouts: 3.53 us -> 0.01 us
    ppermute x15 -> x17, waiting for transfers between devices: 18.9 us -> 15.6 us  [swap(): return lax.ppermute(value, both, [(i, i ^ mask) for i in range(total)])]
    unnamed x1 -> x0, other arithmetic: 1.01 us -> none
    mul x0 -> x1, other arithmetic: none -> 1 us  [pair_body(): masked = grad_out * relu_mask.astype(jnp.bfloat16)]
    add x1 -> x3, other arithmetic: 0.03 us -> 0.74 us  [the longest x1 0.68 us: pair_body(): spots = (tile_rows ^ rep_id) * row + (tile_cols ^ row_id)]
    ppermute x15 -> x17, starting transfers between devices: 18.6 us -> 18 us  [swap(): return lax.ppermute(value, both, [(i, i ^ mask) for i in range(total)])]
    pallas_call x1, Pallas kernels: 1.31 us -> 0.76 us  [products(): pl.pallas_call(functools.partial(product_kernel, scale), out_shape=[jax.S...]
  transfers between devices with their start and end apart: 15 -> 17, of which waited for: 9 -> 12; matrix products, arithmetic and copies ran while one was open for 2% -> 4% of each run, Pallas kernels for 5% -> 6%
where the time goes in v2:
time: 41.5 us; the launch traced here: 41.4 us
  starting transfers between devices  18 us (43%)
  waiting for transfers between devices  15.6 us (38%)
  Pallas kernels  3.05 us (7%)
  other arithmetic  2.59 us (6%)
  between operations  1.43 us (3%)
  matrix products  0.83 us (2%)
    ppermute x17, starting transfers between devices, swap(): return lax.ppermute(value, both, [(i, i ^ mask) for i in range(total)])  18 us
    ppermute x17, waiting for transfers between devices, swap(): return lax.ppermute(value, both, [(i, i ^ mask) for i in range(total)])  15.6 us
    pallas_call x1, Pallas kernels, merge_tiles(): pl.pallas_call(functools.partial(merge_kernel, order, group), out_shape=[...  2.28 us
    mul x1, other arithmetic, pair_body(): masked = grad_out * relu_mask.astype(jnp.bfloat16)  1 us
  transfers between devices with their start and end apart: 17, of which 12 were waited for; matrix products, arithmetic and copies ran while one was open for 4% of the time, Pallas kernels for 6%

profile of v2, /device:TPU:0, one launch (start us, length us, event | category | flops | bytes accessed | tf_op | source)
XLA Modules:
  0.0 41.4 jit_solution(10842104762153807832)
XLA Ops:
  0.7 1.0 %convert_multiply_fusion = bf16[128,256]{1,0:T(8,128)(2,1)S(1)} fusion(bf16[128,256]{1,0:T(8,128)(2,1)} %param.8, s32[128,256]{1,0:T(8,128)} %param.9), kind=kLoop, calls=%fused_computation.12 | loop fusion | flops 65536 | bytes 262144 | tf_op jit(solution)/shard_map/mul | solution.py:175
  1.7 5.1 %collective-permute-start = (bf16[128,256]{1,0:T(8,128)(2,1)S(1)}, bf16[128,256]{1,0:T(8,128)(2,1)S(1)}, u32[]{:S(2)}, u32[]{:S(2)}) collective-permute-start(bf16[128,256]{1,0:T(8,128)(2,1)S(1)} %convert_multiply_fusion), channel_id=1, source_target_pairs={{0,12},{1,13},{2,14},{3,15},{4,8},{5,9},{6,10},{7,11},{8,4},{9,5},... | collective-permute-start | bytes 196616 | tf_op jit(solution)/shard_map/ppermute | solution.py:62
  6.8 0.6 %collective-permute-start.2 = (bf16[128,256]{1,0:T(8,128)(2,1)S(1)}, bf16[128,256]{1,0:T(8,128)(2,1)S(1)}, u32[]{:S(2)}, u32[]{:S(2)}) collective-permute-start(bf16[128,256]{1,0:T(8,128)(2,1)S(1)} %convert_multiply_fusion), channel_id=1, source_target_pairs={{0,4},{1,5},{2,6},{3,7},{4,0},{5,1},{6,2},{7,3},{8,12},{9,13},{10,... | collective-permute-start | bytes 196616 | tf_op jit(solution)/shard_map/ppermute | solution.py:62
  8.1 0.7 %xor_add_fusion = s32[128]{0:T(128)S(1)} fusion(s32[128]{0:T(128)} %param.14, s32[128]{0:T(128)} %param.13, s32[]{:T(128)S(6)} %axis_index.22, s32[]{:T(128)S(6)} %axis_index.25), kind=kLoop, calls=%fused_computation.14 | loop fusion | flops 512 | bytes 1544 | tf_op jit(solution)/shard_map/add | solution.py:183
  8.8 2.3 %shard_map.95 = (bf16[256,1024]{1,0:T(8,128)(2,1)S(1)}, bf16[256,1024]{1,0:T(8,128)(2,1)S(1)}) custom-call(s32[129]{0:T(256)S(1)} %pad_add_fusion.spots_ref, bf16[128,128,128]{2,1,0:T(8,128)(2,1)} %values_ref.1), custom_call_target="tpu_custom_call" | custom-call | flops 2097152 | bytes 8388608 | tf_op jit(solution)/shard_map/pallas_call | solution.py:115
  11.1 1.3 %collective-permute-done.1 = bf16[128,256]{1,0:T(8,128)(2,1)S(1)} collective-permute-done((bf16[128,256]{1,0:T(8,128)(2,1)S(1)}, bf16[128,256]{1,0:T(8,128)(2,1)S(1)}, u32[]{:S(2)}, u32[]{:S(2)}) %collective-permute-start.1) | collective-permute-done | bytes 65568 | tf_op jit(solution)/shard_map/ppermute | solution.py:62
  12.5 1.6 %collective-permute-start.3 = (bf16[512,256]{1,0:T(8,128)(2,1)S(1)}, bf16[512,256]{1,0:T(8,128)(2,1)S(1)}, u32[]{:S(2)}, u32[]{:S(2)}) collective-permute-start(bf16[512,256]{1,0:T(8,128)(2,1)S(1)} %pad_maximum_fusion.1), channel_id=1, source_target_pairs={{0,2},{1,3},{2,0},{3,1},{4,6},{5,7},{6,4},{7,5},{8,10},{9,11},{10,... | collective-permute-start | bytes 786440 | tf_op jit(solution)/shard_map/ppermute | solution.py:62
  14.1 1.5 %collective-permute-start.4 = (bf16[128,256]{1,0:T(8,128)(2,1)S(1)}, bf16[128,256]{1,0:T(8,128)(2,1)S(1)}, u32[]{:S(2)}, u32[]{:S(2)}) collective-permute-start(bf16[128,256]{1,0:T(8,128)(2,1)S(1)} %copy-done.1), channel_id=1, source_target_pairs={{0,16},{1,17},{2,18},{3,19},{4,20},{5,21},{6,22},{7,23},{8,24},{9,... | collective-permute-start | bytes 196616 | tf_op jit(solution)/shard_map/ppermute | solution.py:62
  15.6 2.8 %collective-permute-done.4 = bf16[128,256]{1,0:T(8,128)(2,1)S(1)} collective-permute-done((bf16[128,256]{1,0:T(8,128)(2,1)S(1)}, bf16[128,256]{1,0:T(8,128)(2,1)S(1)}, u32[]{:S(2)}, u32[]{:S(2)}) %collective-permute-start.4) | collective-permute-done | bytes 65568 | tf_op jit(solution)/shard_map/ppermute | solution.py:62
  18.5 2.8 %collective-permute-done.3 = bf16[512,256]{1,0:T(8,128)(2,1)S(1)} collective-permute-done((bf16[512,256]{1,0:T(8,128)(2,1)S(1)}, bf16[512,256]{1,0:T(8,128)(2,1)S(1)}, u32[]{:S(2)}, u32[]{:S(2)}) %collective-permute-start.3) | collective-permute-done | bytes 262176 | tf_op jit(solution)/shard_map/ppermute | solution.py:62
  21.3 0.8 %shard_map.96 = (f32[128,256]{1,0:T(8,128)S(1)}, f32[128,256]{1,0:T(8,128)S(1)}, f32[256,256]{1,0:T(8,128)S(1)}, bf16[256,256]{1,0:T(8,128)(2,1)S(1)}) custom-call(s32[1]{0:T(128)} %bitcast.place_ref, bf16[256,1024]{1,0:T(8,128)(2,1)S(1)} %get-tuple-element.20.own_tiles_ref, bf16[256,1024]{1,0:T(8,128)(2,1)S(1)} %collective-permute-done.5.twin_tiles_ref, ...), custom_call_target="tpu_custom_call" | custom-call | flops 268435456 | bytes 1048576 | tf_op jit(solution)/shard_map/pallas_call | solution.py:148
  22.1 1.3 %collective-permute-done.9 = f32[128,256]{1,0:T(8,128)S(1)} collective-permute-done((f32[128,256]{1,0:T(8,128)S(1)}, f32[128,256]{1,0:T(8,128)S(1)}, u32[]{:S(2)}, u32[]{:S(2)}) %collective-permute-start.9) | collective-permute-done | bytes 131104 | tf_op jit(solution)/shard_map/ppermute | solution.py:62
  23.5 2.5 %collective-permute-start.10 = (bf16[128,256]{1,0:T(8,128)(2,1)S(1)}, bf16[128,256]{1,0:T(8,128)(2,1)S(1)}, u32[]{:S(2)}, u32[]{:S(2)}) collective-permute-start(bf16[128,256]{1,0:T(8,128)(2,1)S(1)} %add_convert_fusion.1), channel_id=1, source_target_pairs={{0,18},{1,19},{2,16},{3,17},{4,22},{5,23},{6,20},{7,21},{8,26},{9,... | collective-permute-start | bytes 196616 | tf_op jit(solution)/shard_map/ppermute | solution.py:62
  26.0 0.5 %collective-permute-start.11 = (bf16[128,256]{1,0:T(8,128)(2,1)S(1)}, bf16[128,256]{1,0:T(8,128)(2,1)S(1)}, u32[]{:S(2)}, u32[]{:S(2)}) collective-permute-start(bf16[128,256]{1,0:T(8,128)(2,1)S(1)} %add_convert_fusion.1), channel_id=1, source_target_pairs={{0,2},{1,3},{2,0},{3,1},{4,6},{5,7},{6,4},{7,5},{8,10},{9,11},{10,... | collective-permute-start | bytes 196616 | tf_op jit(solution)/shard_map/ppermute | solution.py:62
  26.5 0.5 %collective-permute-start.12 = (bf16[128,256]{1,0:T(8,128)(2,1)S(1)}, bf16[128,256]{1,0:T(8,128)(2,1)S(1)}, u32[]{:S(2)}, u32[]{:S(2)}) collective-permute-start(bf16[128,256]{1,0:T(8,128)(2,1)S(1)} %add_convert_fusion.1), channel_id=1, source_target_pairs={{0,16},{1,17},{2,18},{3,19},{4,20},{5,21},{6,22},{7,23},{8,24},{9,... | collective-permute-start | bytes 196616 | tf_op jit(solution)/shard_map/ppermute | solution.py:62
  27.0 1.7 %collective-permute-done.10 = bf16[128,256]{1,0:T(8,128)(2,1)S(1)} collective-permute-done((bf16[128,256]{1,0:T(8,128)(2,1)S(1)}, bf16[128,256]{1,0:T(8,128)(2,1)S(1)}, u32[]{:S(2)}, u32[]{:S(2)}) %collective-permute-start.10) | collective-permute-done | bytes 65568 | tf_op jit(solution)/shard_map/ppermute | solution.py:62
  28.7 1.5 %collective-permute-done.11 = bf16[128,256]{1,0:T(8,128)(2,1)S(1)} collective-permute-done((bf16[128,256]{1,0:T(8,128)(2,1)S(1)}, bf16[128,256]{1,0:T(8,128)(2,1)S(1)}, u32[]{:S(2)}, u32[]{:S(2)}) %collective-permute-start.11) | collective-permute-done | bytes 65568 | tf_op jit(solution)/shard_map/ppermute | solution.py:62
  30.8 3.1 %collective-permute-start.13 = (bf16[128,256]{1,0:T(8,128)(2,1)S(1)}, bf16[128,256]{1,0:T(8,128)(2,1)S(1)}, u32[]{:S(2)}, u32[]{:S(2)}) collective-permute-start(bf16[128,256]{1,0:T(8,128)(2,1)S(1)} %add_convert_fusion), channel_id=1, source_target_pairs={{0,12},{1,13},{2,14},{3,15},{4,8},{5,9},{6,10},{7,11},{8,4},{9,5},... | collective-permute-start | bytes 196616 | tf_op jit(solution)/shard_map/ppermute | solution.py:62
  33.9 1.4 %collective-permute-start.15 = (bf16[128,256]{1,0:T(8,128)(2,1)S(1)}, bf16[128,256]{1,0:T(8,128)(2,1)S(1)}, u32[]{:S(2)}, u32[]{:S(2)}) collective-permute-start(bf16[128,256]{1,0:T(8,128)(2,1)S(1)} %add_convert_fusion), channel_id=1, source_target_pairs={{0,4},{1,5},{2,6},{3,7},{4,0},{5,1},{6,2},{7,3},{8,12},{9,13},{10,... | collective-permute-start | bytes 196616 | tf_op jit(solution)/shard_map/ppermute | solution.py:62
  35.3 0.8 %collective-permute-start.8 = (bf16[128,256]{1,0:T(8,128)(2,1)S(1)}, bf16[128,256]{1,0:T(8,128)(2,1)S(1)}, u32[]{:S(2)}, u32[]{:S(2)}) collective-permute-start(bf16[128,256]{1,0:T(8,128)(2,1)S(1)} %slice.16), channel_id=1, source_target_pairs={{0,16},{1,17},{2,18},{3,19},{4,20},{5,21},{6,22},{7,23},{8,24},{9,... | collective-permute-start | bytes 196616 | tf_op jit(solution)/shard_map/ppermute | solution.py:62
  36.1 0.9 %collective-permute-done.13 = bf16[128,256]{1,0:T(8,128)(2,1)S(1)} collective-permute-done((bf16[128,256]{1,0:T(8,128)(2,1)S(1)}, bf16[128,256]{1,0:T(8,128)(2,1)S(1)}, u32[]{:S(2)}, u32[]{:S(2)}) %collective-permute-start.13) | collective-permute-done | bytes 65568 | tf_op jit(solution)/shard_map/ppermute | solution.py:62
  37.0 2.1 %collective-permute-done.14 = bf16[128,256]{1,0:T(8,128)(2,1)S(1)} collective-permute-done((bf16[128,256]{1,0:T(8,128)(2,1)S(1)}, bf16[128,256]{1,0:T(8,128)(2,1)S(1)}, u32[]{:S(2)}, u32[]{:S(2)}) %collective-permute-start.14) | collective-permute-done | bytes 65568 | tf_op jit(solution)/shard_map/ppermute | solution.py:62
  39.6 0.8 %convolution_convert_fusion = bf16[128,256]{1,0:T(8,128)(2,1)} fusion(bf16[256,256]{1,0:T(8,128)(2,1)S(1)} %copy-done, f32[256,256]{1,0:T(8,128)S(1)} %convert_add_fusion, bf16[128,256]{1,0:T(8,128)(2,1)S(1)} %collective-permute-done.8), kind=kOutput, calls=%fused_computation | convolution fusion | flops 16908288 | bytes 393216 | tf_op jit(solution)/shard_map/dot_general | solution.py:209
  40.7 0.7 %maximum_select_fusion = f32[256,256]{1,0:T(8,128)} fusion(f32[128,256]{1,0:T(8,128)S(1)} %collective-permute-done.16, f32[128,256]{1,0:T(8,128)S(1)} %add_add_fusion, pred[]{:T(512)S(6)} %eq.5), kind=kLoop, calls=%fused_computation.3 | loop fusion | flops 196608 | bytes 524289 | tf_op jit(solution)/shard_map/jit(_where)/select_n | solution.py:204
  (29 shorter events, 1.7 us)
Async XLA Ops:
  0.6 39.0 %copy-start = (bf16[256,256]{1,0:T(8,128)(2,1)S(1)}, bf16[256,256]{1,0:T(8,128)(2,1)}, u32[]{:S(2)}) copy-start(bf16[256,256]{1,0:T(8,128)(2,1)} %param.11) | copy-start | bytes 393220
  0.6 13.4 %copy-start.1 = (bf16[128,256]{1,0:T(8,128)(2,1)S(1)}, bf16[128,256]{1,0:T(8,128)(2,1)}, u32[]{:S(2)}) copy-start(bf16[128,256]{1,0:T(8,128)(2,1)} %param.10) | copy-start | bytes 196612
  1.7 9.4 %collective-permute-start = (bf16[128,256]{1,0:T(8,128)(2,1)S(1)}, bf16[128,256]{1,0:T(8,128)(2,1)S(1)}, u32[]{:S(2)}, u32[]{:S(2)}) collective-permute-start(bf16[128,256]{1,0:T(8,128)(2,1)S(1)} %convert_multiply_fusion), channel_id=1, source_target_pairs={{0,12},{1,13},{2,14},{3,15},{4,8},{5,9},{6,10},{7,11},{8,4},{9,5},... | collective-permute-start | bytes 196616 | tf_op jit(solution)/shard_map/ppermute | solution.py:62
  6.8 5.6 %collective-permute-start.1 = (bf16[128,256]{1,0:T(8,128)(2,1)S(1)}, bf16[128,256]{1,0:T(8,128)(2,1)S(1)}, u32[]{:S(2)}, u32[]{:S(2)}) collective-permute-start(bf16[128,256]{1,0:T(8,128)(2,1)S(1)} %convert_multiply_fusion), channel_id=1, source_target_pairs={{0,8},{1,9},{2,10},{3,11},{4,12},{5,13},{6,14},{7,15},{8,0},{9,1},... | collective-permute-start | bytes 196616 | tf_op jit(solution)/shard_map/ppermute | solution.py:62
  6.8 5.6 %collective-permute-start.2 = (bf16[128,256]{1,0:T(8,128)(2,1)S(1)}, bf16[128,256]{1,0:T(8,128)(2,1)S(1)}, u32[]{:S(2)}, u32[]{:S(2)}) collective-permute-start(bf16[128,256]{1,0:T(8,128)(2,1)S(1)} %convert_multiply_fusion), channel_id=1, source_target_pairs={{0,4},{1,5},{2,6},{3,7},{4,0},{5,1},{6,2},{7,3},{8,12},{9,13},{10,... | collective-permute-start | bytes 196616 | tf_op jit(solution)/shard_map/ppermute | solution.py:62
  12.4 5.9 %collective-permute-start.5 = (bf16[256,1024]{1,0:T(8,128)(2,1)S(1)}, bf16[256,1024]{1,0:T(8,128)(2,1)S(1)}, u32[]{:S(2)}, u32[]{:S(2)}) collective-permute-start(bf16[256,1024]{1,0:T(8,128)(2,1)S(1)} %get-tuple-element.23), channel_id=1, source_target_pairs={{0,1},{1,0},{2,3},{3,2},{4,5},{5,4},{6,7},{7,6},{8,9},{9,8},{10,11... | collective-permute-start | bytes 1572872 | tf_op jit(solution)/shard_map/ppermute | solution.py:62
  12.5 8.7 %collective-permute-start.3 = (bf16[512,256]{1,0:T(8,128)(2,1)S(1)}, bf16[512,256]{1,0:T(8,128)(2,1)S(1)}, u32[]{:S(2)}, u32[]{:S(2)}) collective-permute-start(bf16[512,256]{1,0:T(8,128)(2,1)S(1)} %pad_maximum_fusion.1), channel_id=1, source_target_pairs={{0,2},{1,3},{2,0},{3,1},{4,6},{5,7},{6,4},{7,5},{8,10},{9,11},{10,... | collective-permute-start | bytes 786440 | tf_op jit(solution)/shard_map/ppermute | solution.py:62
  14.1 4.3 %collective-permute-start.4 = (bf16[128,256]{1,0:T(8,128)(2,1)S(1)}, bf16[128,256]{1,0:T(8,128)(2,1)S(1)}, u32[]{:S(2)}, u32[]{:S(2)}) collective-permute-start(bf16[128,256]{1,0:T(8,128)(2,1)S(1)} %copy-done.1), channel_id=1, source_target_pairs={{0,16},{1,17},{2,18},{3,19},{4,20},{5,21},{6,22},{7,23},{8,24},{9,... | collective-permute-start | bytes 196616 | tf_op jit(solution)/shard_map/ppermute | solution.py:62
  18.4 2.9 %collective-permute-start.6 = (bf16[256,256]{1,0:T(8,128)(2,1)S(1)}, bf16[256,256]{1,0:T(8,128)(2,1)S(1)}, u32[]{:S(2)}, u32[]{:S(2)}) collective-permute-start(bf16[256,256]{1,0:T(8,128)(2,1)S(1)} %pad_maximum_fusion.2.own_in_ref), channel_id=1, source_target_pairs={{0,1},{1,0},{2,3},{3,2},{4,5},{5,4},{6,7},{7,6},{8,9},{9,8},{10,11... | collective-permute-start | bytes 393224 | tf_op jit(solution)/shard_map/ppermute | solution.py:62
  22.0 1.4 %collective-permute-start.9 = (f32[128,256]{1,0:T(8,128)S(1)}, f32[128,256]{1,0:T(8,128)S(1)}, u32[]{:S(2)}, u32[]{:S(2)}) collective-permute-start(f32[128,256]{1,0:T(8,128)S(1)} %get-tuple-element.33), channel_id=1, source_target_pairs={{0,1},{1,0},{2,3},{3,2},{4,5},{5,4},{6,7},{7,6},{8,9},{9,8},{10,11... | collective-permute-start | bytes 393224 | tf_op jit(solution)/shard_map/ppermute | solution.py:62
  23.5 5.3 %collective-permute-start.10 = (bf16[128,256]{1,0:T(8,128)(2,1)S(1)}, bf16[128,256]{1,0:T(8,128)(2,1)S(1)}, u32[]{:S(2)}, u32[]{:S(2)}) collective-permute-start(bf16[128,256]{1,0:T(8,128)(2,1)S(1)} %add_convert_fusion.1), channel_id=1, source_target_pairs={{0,18},{1,19},{2,16},{3,17},{4,22},{5,23},{6,20},{7,21},{8,26},{9,... | collective-permute-start | bytes 196616 | tf_op jit(solution)/shard_map/ppermute | solution.py:62
  26.0 4.3 %collective-permute-start.11 = (bf16[128,256]{1,0:T(8,128)(2,1)S(1)}, bf16[128,256]{1,0:T(8,128)(2,1)S(1)}, u32[]{:S(2)}, u32[]{:S(2)}) collective-permute-start(bf16[128,256]{1,0:T(8,128)(2,1)S(1)} %add_convert_fusion.1), channel_id=1, source_target_pairs={{0,2},{1,3},{2,0},{3,1},{4,6},{5,7},{6,4},{7,5},{8,10},{9,11},{10,... | collective-permute-start | bytes 196616 | tf_op jit(solution)/shard_map/ppermute | solution.py:62
  26.5 4.3 %collective-permute-start.12 = (bf16[128,256]{1,0:T(8,128)(2,1)S(1)}, bf16[128,256]{1,0:T(8,128)(2,1)S(1)}, u32[]{:S(2)}, u32[]{:S(2)}) collective-permute-start(bf16[128,256]{1,0:T(8,128)(2,1)S(1)} %add_convert_fusion.1), channel_id=1, source_target_pairs={{0,16},{1,17},{2,18},{3,19},{4,20},{5,21},{6,22},{7,23},{8,24},{9,... | collective-permute-start | bytes 196616 | tf_op jit(solution)/shard_map/ppermute | solution.py:62
  27.0 8.2 %collective-permute-start.7 = (bf16[256,256]{1,0:T(8,128)(2,1)S(1)}, bf16[256,256]{1,0:T(8,128)(2,1)S(1)}, u32[]{:S(2)}, u32[]{:S(2)}) collective-permute-start(bf16[256,256]{1,0:T(8,128)(2,1)S(1)} %get-tuple-element.31), channel_id=1, source_target_pairs={{0,1},{1,0},{2,3},{3,2},{4,5},{5,4},{6,7},{7,6},{8,9},{9,8},{10,11... | collective-permute-start | bytes 393224 | tf_op jit(solution)/shard_map/ppermute | solution.py:62
  30.8 6.2 %collective-permute-start.13 = (bf16[128,256]{1,0:T(8,128)(2,1)S(1)}, bf16[128,256]{1,0:T(8,128)(2,1)S(1)}, u32[]{:S(2)}, u32[]{:S(2)}) collective-permute-start(bf16[128,256]{1,0:T(8,128)(2,1)S(1)} %add_convert_fusion), channel_id=1, source_target_pairs={{0,12},{1,13},{2,14},{3,15},{4,8},{5,9},{6,10},{7,11},{8,4},{9,5},... | collective-permute-start | bytes 196616 | tf_op jit(solution)/shard_map/ppermute | solution.py:62
  33.9 5.2 %collective-permute-start.14 = (bf16[128,256]{1,0:T(8,128)(2,1)S(1)}, bf16[128,256]{1,0:T(8,128)(2,1)S(1)}, u32[]{:S(2)}, u32[]{:S(2)}) collective-permute-start(bf16[128,256]{1,0:T(8,128)(2,1)S(1)} %add_convert_fusion), channel_id=1, source_target_pairs={{0,8},{1,9},{2,10},{3,11},{4,12},{5,13},{6,14},{7,15},{8,0},{9,1},... | collective-permute-start | bytes 196616 | tf_op jit(solution)/shard_map/ppermute | solution.py:62
  33.9 5.4 %collective-permute-start.15 = (bf16[128,256]{1,0:T(8,128)(2,1)S(1)}, bf16[128,256]{1,0:T(8,128)(2,1)S(1)}, u32[]{:S(2)}, u32[]{:S(2)}) collective-permute-start(bf16[128,256]{1,0:T(8,128)(2,1)S(1)} %add_convert_fusion), channel_id=1, source_target_pairs={{0,4},{1,5},{2,6},{3,7},{4,0},{5,1},{6,2},{7,3},{8,12},{9,13},{10,... | collective-permute-start | bytes 196616 | tf_op jit(solution)/shard_map/ppermute | solution.py:62
  35.3 4.3 %collective-permute-start.8 = (bf16[128,256]{1,0:T(8,128)(2,1)S(1)}, bf16[128,256]{1,0:T(8,128)(2,1)S(1)}, u32[]{:S(2)}, u32[]{:S(2)}) collective-permute-start(bf16[128,256]{1,0:T(8,128)(2,1)S(1)} %slice.16), channel_id=1, source_target_pairs={{0,16},{1,17},{2,18},{3,19},{4,20},{5,21},{6,22},{7,23},{8,24},{9,... | collective-permute-start | bytes 196616 | tf_op jit(solution)/shard_map/ppermute | solution.py:62
  39.3 1.4 %collective-permute-start.16 = (f32[128,256]{1,0:T(8,128)S(1)}, f32[128,256]{1,0:T(8,128)S(1)}, u32[]{:S(2)}, u32[]{:S(2)}) collective-permute-start(f32[128,256]{1,0:T(8,128)S(1)} %add_add_fusion), channel_id=1, source_target_pairs={{0,1},{1,0},{2,3},{3,2},{4,5},{5,4},{6,7},{7,6},{8,9},{9,8},{10,11... | collective-permute-start | bytes 393224 | tf_op jit(solution)/shard_map/ppermute | solution.py:62

commit v3 on v2

--- a/solution.py
+++ b/solution.py
@@ -160,10 +160,14 @@
     )(place, own_tiles, twin_tiles, near, own_in, twin_in)
 
 
+def core_swap(value, masks, total):
+    return lax.ppermute(value, both, [(i, i ^ masks[i % 2]) for i in range(total)])
+
+
 def quad_sum(value, low, high, total):
-    third = swap(value, low | high, total)
-    second = swap(value, high, total)
-    first = swap(value, low, total)
+    third = core_swap(value, [a | b for a, b in zip(low, high)], total)
+    second = core_swap(value, high, total)
+    first = core_swap(value, low, total)
     f32 = jnp.float32
     return (third.astype(f32) + second.astype(f32)) + (first.astype(f32) + value.astype(f32))
 
@@ -184,28 +188,30 @@
     spots = jnp.concatenate([spots, tile_count])
     order = order + [o + 2 for o in order]
     order = order + [o + 1 for o in order]
+    other_in = swap(layer_input, row, total)
     own_tiles, far_tiles = merge_tiles(spots, tile_values, order, rep)
-    near, own_tiles, far_tiles, own_in = lax.optimization_barrier((near, own_tiles, far_tiles, layer_input))
+    other_in, own_tiles, far_tiles, near = lax.optimization_barrier((other_in, own_tiles, far_tiles, near))
     near = jnp.concatenate([near, swap(near, 2, total)], 0)
-    own_in = jnp.concatenate([own_in, swap(own_in, row, total)], 0)
-    twin_tiles = swap(far_tiles, 1, total)
-    own_in, twin_tiles = lax.optimization_barrier((own_in, twin_tiles))
+    own_in = jnp.concatenate([layer_input, other_in], 0)
+    rows = far_tiles.shape[0] // 2
+    twin_tiles = jnp.concatenate([swap(far_tiles[i * rows:(i + 1) * rows], 1, total) for i in range(2)], 0)
     twin_in = swap(own_in, 1, total)
     near, own_in, twin_in, twin_tiles = lax.optimization_barrier((near, own_in, twin_in, twin_tiles))
     keep, send, own, twin = products(place, own_tiles, twin_tiles, near, own_in, twin_in, 1.0 / (blk * total) ** 0.5)
 
     part = (keep + swap(send, 1, total)).astype(jnp.bfloat16)
     part = lax.optimization_barrier(part)
-    part = quad_sum(part, row, top // 2, total).astype(jnp.bfloat16)
+    part = quad_sum(part, (top, row), (2 * top, top // 2), total).astype(jnp.bfloat16)
     part = lax.optimization_barrier(part)
-    part = quad_sum(part, top, 2 * top, total)
+    part = quad_sum(part, (row, top), (top // 2, 2 * top), total)
     part = lax.optimization_barrier(part)
     other = swap(part, 1, total)
     grad_weight = jnp.where(core_id == 0, jnp.concatenate([part, other], 0), jnp.concatenate([other, part], 0))
 
-    own = own + swap(twin, 1, total).astype(jnp.float32)
-    peer = swap(own[blk:].astype(jnp.bfloat16), row, total)
-    prop = (own[:blk] + peer.astype(jnp.float32)).astype(jnp.bfloat16)
+    cross = jnp.concatenate([own[blk:].astype(jnp.bfloat16), twin[blk:]], 0)
+    cross = swap(cross, row, total).astype(jnp.float32)
+    twin = (twin[:blk].astype(jnp.float32) + cross[blk:]).astype(jnp.bfloat16)
+    prop = (own[:blk] + cross[:blk] + swap(twin, 1, total).astype(jnp.float32)).astype(jnp.bfloat16)
     grad_input = lax.dot_general(
         prop, weight, (((1,), (1,)), ((), ())), preferred_element_type=jnp.float32
     ).astype(jnp.bfloat16)

time: 41.5 us -> 40.4 us (0.973)
  waiting for transfers between devices: 15.6 us -> 12.6 us
  starting transfers between devices: 18 us -> 19.3 us
    ppermute x17 -> x12, waiting for transfers between devices: 15.6 us -> 5.82 us  [swap(): return lax.ppermute(value, both, [(i, i ^ mask) for i in range(total)])]
    ppermute x0 -> x6, starting transfers between devices: none -> 8.01 us  [core_swap(): lax.ppermute(value, both, [(i, i ^ masks[i % 2]) for i in range(total)])]
    ppermute x0 -> x6, waiting for transfers between devices: none -> 6.77 us  [core_swap(): lax.ppermute(value, both, [(i, i ^ masks[i % 2]) for i in range(total)])]
    ppermute x17 -> x12, starting transfers between devices: 18 us -> 11.3 us  [swap(): return lax.ppermute(value, both, [(i, i ^ mask) for i in range(total)])]
  transfers between devices with their start and end apart: 17 -> 18, of which waited for: 12 -> 7; matrix products, arithmetic and copies ran while one was open for 4% -> 4% of each run, Pallas kernels for 6% -> 6%
where the time goes in v3:
time: 40.4 us; the launch traced here: 40.3 us
  starting transfers between devices  19.3 us (48%)
  waiting for transfers between devices  12.6 us (31%)
  Pallas kernels  3.29 us (8%)
  other arithmetic  2.64 us (7%)
  between operations  1.52 us (4%)
  matrix products  0.83 us (2%)
    ppermute x12, starting transfers between devices, swap(): return lax.ppermute(value, both, [(i, i ^ mask) for i in range(total)])  11.3 us
    ppermute x6, starting transfers between devices, core_swap(): lax.ppermute(value, both, [(i, i ^ masks[i % 2]) for i in range(total)])  8.01 us
    ppermute x6, waiting for transfers between devices, core_swap(): lax.ppermute(value, both, [(i, i ^ masks[i % 2]) for i in range(total)])  6.77 us
    ppermute x12, waiting for transfers between devices, swap(): return lax.ppermute(value, both, [(i, i ^ mask) for i in range(total)])  5.82 us
    pallas_call x1, Pallas kernels, merge_tiles(): pl.pallas_call(functools.partial(merge_kernel, order, group), out_shape=[...  2.53 us
    mul x1, other arithmetic, pair_body(): masked = grad_out * relu_mask.astype(jnp.bfloat16)  1 us
    dot_general x1, matrix products, pair_body(): lax.dot_general(prop, weight, (((1,), (1,)), ((), ())), preferred_element...  0.83 us
  transfers between devices with their start and end apart: 18, of which 7 were waited for; matrix products, arithmetic and copies ran while one was open for 4% of the time, Pallas kernels for 6%

profile of v3, /device:TPU:0, one launch (start us, length us, event | category | flops | bytes accessed | tf_op | source)
XLA Modules:
  0.0 40.3 jit_solution(4977550331543804663)
XLA Ops:
  0.7 1.0 %convert_multiply_fusion = bf16[128,256]{1,0:T(8,128)(2,1)S(1)} fusion(bf16[128,256]{1,0:T(8,128)(2,1)} %param.8, s32[128,256]{1,0:T(8,128)} %param.9), kind=kLoop, calls=%fused_computation.15 | loop fusion | flops 65536 | bytes 262144 | tf_op jit(solution)/shard_map/mul | solution.py:179
  1.7 5.1 %collective-permute-start.1 = (bf16[128,256]{1,0:T(8,128)(2,1)S(1)}, bf16[128,256]{1,0:T(8,128)(2,1)S(1)}, u32[]{:S(2)}, u32[]{:S(2)}) collective-permute-start(bf16[128,256]{1,0:T(8,128)(2,1)S(1)} %convert_multiply_fusion), channel_id=1, source_target_pairs={{0,12},{1,13},{2,14},{3,15},{4,8},{5,9},{6,10},{7,11},{8,4},{9,5},... | collective-permute-start | bytes 196616 | tf_op jit(solution)/shard_map/ppermute | solution.py:62
  6.8 0.6 %collective-permute-start.3 = (bf16[128,256]{1,0:T(8,128)(2,1)S(1)}, bf16[128,256]{1,0:T(8,128)(2,1)S(1)}, u32[]{:S(2)}, u32[]{:S(2)}) collective-permute-start(bf16[128,256]{1,0:T(8,128)(2,1)S(1)} %convert_multiply_fusion), channel_id=1, source_target_pairs={{0,4},{1,5},{2,6},{3,7},{4,0},{5,1},{6,2},{7,3},{8,12},{9,13},{10,... | collective-permute-start | bytes 196616 | tf_op jit(solution)/shard_map/ppermute | solution.py:62
  7.4 1.6 %collective-permute-start = (bf16[128,256]{1,0:T(8,128)(2,1)}, bf16[128,256]{1,0:T(8,128)(2,1)S(1)}, u32[]{:S(2)}, u32[]{:S(2)}) collective-permute-start(bf16[128,256]{1,0:T(8,128)(2,1)} %param.10), channel_id=1, source_target_pairs={{0,16},{1,17},{2,18},{3,19},{4,20},{5,21},{6,22},{7,23},{8,24},{9,... | collective-permute-start | bytes 196616 | tf_op jit(solution)/shard_map/ppermute | solution.py:62
  9.7 0.7 %xor_add_fusion = s32[128]{0:T(128)S(1)} fusion(s32[128]{0:T(128)} %param.14, s32[128]{0:T(128)} %param.13, s32[]{:T(128)S(6)} %axis_index.22, s32[]{:T(128)S(6)} %axis_index.25), kind=kLoop, calls=%fused_computation.19 | loop fusion | flops 512 | bytes 1544 | tf_op jit(solution)/shard_map/add | solution.py:187
  10.4 2.5 %shard_map.95 = (bf16[256,1024]{1,0:T(8,128)(2,1)S(1)}, bf16[256,1024]{1,0:T(8,128)(2,1)S(1)}) custom-call(s32[129]{0:T(256)S(1)} %pad_add_fusion.spots_ref, bf16[128,128,128]{2,1,0:T(8,128)(2,1)} %values_ref.1), custom_call_target="tpu_custom_call" | custom-call | flops 2097152 | bytes 8388608 | tf_op jit(solution)/shard_map/pallas_call | solution.py:115
  13.0 1.3 %collective-permute-start.4 = (bf16[512,256]{1,0:T(8,128)(2,1)S(1)}, bf16[512,256]{1,0:T(8,128)(2,1)S(1)}, u32[]{:S(2)}, u32[]{:S(2)}) collective-permute-start(bf16[512,256]{1,0:T(8,128)(2,1)S(1)} %pad_maximum_fusion.2), channel_id=1, source_target_pairs={{0,2},{1,3},{2,0},{3,1},{4,6},{5,7},{6,4},{7,5},{8,10},{9,11},{10,... | collective-permute-start | bytes 786440 | tf_op jit(solution)/shard_map/ppermute | solution.py:62
  14.4 0.5 %collective-permute-start.7 = (bf16[128,1024]{1,0:T(8,128)(2,1)S(1)}, bf16[128,1024]{1,0:T(8,128)(2,1)S(1)}, u32[]{:S(2)}, u32[]{:S(2)}) collective-permute-start(bf16[128,1024]{1,0:T(8,128)(2,1)S(1)} %get-tuple-element.31), channel_id=1, source_target_pairs={{0,1},{1,0},{2,3},{3,2},{4,5},{5,4},{6,7},{7,6},{8,9},{9,8},{10,11... | collective-permute-start | bytes 786440 | tf_op jit(solution)/shard_map/ppermute | solution.py:62
  15.1 5.3 %collective-permute-done.4 = bf16[512,256]{1,0:T(8,128)(2,1)S(1)} collective-permute-done((bf16[512,256]{1,0:T(8,128)(2,1)S(1)}, bf16[512,256]{1,0:T(8,128)(2,1)S(1)}, u32[]{:S(2)}, u32[]{:S(2)}) %collective-permute-start.4) | collective-permute-done | bytes 262176 | tf_op jit(solution)/shard_map/ppermute | solution.py:62
  20.5 0.8 %shard_map.96 = (f32[128,256]{1,0:T(8,128)S(1)}, f32[128,256]{1,0:T(8,128)S(1)}, f32[256,256]{1,0:T(8,128)S(1)}, bf16[256,256]{1,0:T(8,128)(2,1)S(1)}) custom-call(s32[1]{0:T(128)} %bitcast.place_ref, bf16[256,1024]{1,0:T(8,128)(2,1)S(1)} %get-tuple-element.18.own_tiles_ref, bf16[256,1024]{1,0:T(8,128)(2,1)S(1)} %pad_maximum_fusion.1.twin_tiles_ref, ...), custom_call_target="tpu_custom_call" | custom-call | flops 268435456 | bytes 1048576 | tf_op jit(solution)/shard_map/pallas_call | solution.py:148
  21.4 1.7 %collective-permute-start.8 = (bf16[256,256]{1,0:T(8,128)(2,1)S(1)}, bf16[256,256]{1,0:T(8,128)(2,1)S(1)}, u32[]{:S(2)}, u32[]{:S(2)}) collective-permute-start(bf16[256,256]{1,0:T(8,128)(2,1)S(1)} %pad_maximum_fusion.3), channel_id=1, source_target_pairs={{0,16},{1,17},{2,18},{3,19},{4,20},{5,21},{6,22},{7,23},{8,24},{9,... | collective-permute-start | bytes 393224 | tf_op jit(solution)/shard_map/ppermute | solution.py:62
  23.1 2.8 %collective-permute-start.11 = (bf16[128,256]{1,0:T(8,128)(2,1)S(1)}, bf16[128,256]{1,0:T(8,128)(2,1)S(1)}, u32[]{:S(2)}, u32[]{:S(2)}) collective-permute-start(bf16[128,256]{1,0:T(8,128)(2,1)S(1)} %add_convert_fusion.1), channel_id=1, source_target_pairs={{0,12},{1,19},{2,14},{3,17},{4,8},{5,23},{6,10},{7,21},{8,4},{9,27... | collective-permute-start | bytes 196616 | tf_op jit(solution)/shard_map/ppermute | solution.py:164
  25.9 1.7 %collective-permute-start.13 = (bf16[128,256]{1,0:T(8,128)(2,1)S(1)}, bf16[128,256]{1,0:T(8,128)(2,1)S(1)}, u32[]{:S(2)}, u32[]{:S(2)}) collective-permute-start(bf16[128,256]{1,0:T(8,128)(2,1)S(1)} %add_convert_fusion.1), channel_id=1, source_target_pairs={{0,4},{1,17},{2,6},{3,19},{4,0},{5,21},{6,2},{7,23},{8,12},{9,25},... | collective-permute-start | bytes 196616 | tf_op jit(solution)/shard_map/ppermute | solution.py:164
  27.7 1.6 %collective-permute-done.11 = bf16[128,256]{1,0:T(8,128)(2,1)S(1)} collective-permute-done((bf16[128,256]{1,0:T(8,128)(2,1)S(1)}, bf16[128,256]{1,0:T(8,128)(2,1)S(1)}, u32[]{:S(2)}, u32[]{:S(2)}) %collective-permute-start.11) | collective-permute-done | bytes 65568 | tf_op jit(solution)/shard_map/ppermute | solution.py:164
  29.3 1.8 %collective-permute-done.12 = bf16[128,256]{1,0:T(8,128)(2,1)S(1)} collective-permute-done((bf16[128,256]{1,0:T(8,128)(2,1)S(1)}, bf16[128,256]{1,0:T(8,128)(2,1)S(1)}, u32[]{:S(2)}, u32[]{:S(2)}) %collective-permute-start.12) | collective-permute-done | bytes 65568 | tf_op jit(solution)/shard_map/ppermute | solution.py:164
  31.1 1.9 %collective-permute-start.14 = (bf16[128,256]{1,0:T(8,128)(2,1)S(1)}, bf16[128,256]{1,0:T(8,128)(2,1)S(1)}, u32[]{:S(2)}, u32[]{:S(2)}) collective-permute-start(bf16[128,256]{1,0:T(8,128)(2,1)S(1)} %add_convert_fusion), channel_id=1, source_target_pairs={{0,18},{1,13},{2,16},{3,15},{4,22},{5,9},{6,20},{7,11},{8,26},{9,5... | collective-permute-start | bytes 196616 | tf_op jit(solution)/shard_map/ppermute | solution.py:164
  33.0 0.8 %collective-permute-start.15 = (bf16[128,256]{1,0:T(8,128)(2,1)S(1)}, bf16[128,256]{1,0:T(8,128)(2,1)S(1)}, u32[]{:S(2)}, u32[]{:S(2)}) collective-permute-start(bf16[128,256]{1,0:T(8,128)(2,1)S(1)} %add_convert_fusion), channel_id=1, source_target_pairs={{0,2},{1,9},{2,0},{3,11},{4,6},{5,13},{6,4},{7,15},{8,10},{9,1},{1... | collective-permute-start | bytes 196616 | tf_op jit(solution)/shard_map/ppermute | solution.py:164
  33.9 0.8 %collective-permute-start.16 = (bf16[128,256]{1,0:T(8,128)(2,1)S(1)}, bf16[128,256]{1,0:T(8,128)(2,1)S(1)}, u32[]{:S(2)}, u32[]{:S(2)}) collective-permute-start(bf16[128,256]{1,0:T(8,128)(2,1)S(1)} %add_convert_fusion), channel_id=1, source_target_pairs={{0,16},{1,5},{2,18},{3,7},{4,20},{5,1},{6,22},{7,3},{8,24},{9,13},... | collective-permute-start | bytes 196616 | tf_op jit(solution)/shard_map/ppermute | solution.py:164
  34.8 1.6 %collective-permute-done.14 = bf16[128,256]{1,0:T(8,128)(2,1)S(1)} collective-permute-done((bf16[128,256]{1,0:T(8,128)(2,1)S(1)}, bf16[128,256]{1,0:T(8,128)(2,1)S(1)}, u32[]{:S(2)}, u32[]{:S(2)}) %collective-permute-start.14) | collective-permute-done | bytes 65568 | tf_op jit(solution)/shard_map/ppermute | solution.py:164
  36.3 0.9 %collective-permute-done.15 = bf16[128,256]{1,0:T(8,128)(2,1)S(1)} collective-permute-done((bf16[128,256]{1,0:T(8,128)(2,1)S(1)}, bf16[128,256]{1,0:T(8,128)(2,1)S(1)}, u32[]{:S(2)}, u32[]{:S(2)}) %collective-permute-start.15) | collective-permute-done | bytes 65568 | tf_op jit(solution)/shard_map/ppermute | solution.py:164
  37.3 0.8 %collective-permute-done.16 = bf16[128,256]{1,0:T(8,128)(2,1)S(1)} collective-permute-done((bf16[128,256]{1,0:T(8,128)(2,1)S(1)}, bf16[128,256]{1,0:T(8,128)(2,1)S(1)}, u32[]{:S(2)}, u32[]{:S(2)}) %collective-permute-start.16) | collective-permute-done | bytes 65568 | tf_op jit(solution)/shard_map/ppermute | solution.py:164
  38.3 0.8 %convolution_convert_fusion = bf16[128,256]{1,0:T(8,128)(2,1)} fusion(bf16[256,256]{1,0:T(8,128)(2,1)S(1)} %copy-done, f32[256,256]{1,0:T(8,128)S(1)} %convert_element_type.53, bf16[128,256]{1,0:T(8,128)(2,1)S(1)} %collective-permute-done.9, f32[256,256]{1,0:T(8,128)S(1)} %get-tuple-element.26), kind=kOutput, calls=%fused_computation | convolution fusion | flops 16941056 | bytes 524288 | tf_op jit(solution)/shard_map/dot_general | solution.py:215
  39.1 0.5 %collective-permute-done.17 = f32[128,256]{1,0:T(8,128)S(1)} collective-permute-done((f32[128,256]{1,0:T(8,128)S(1)}, f32[128,256]{1,0:T(8,128)S(1)}, u32[]{:S(2)}, u32[]{:S(2)}) %collective-permute-start.17) | collective-permute-done | bytes 131104 | tf_op jit(solution)/shard_map/ppermute | solution.py:62
  39.6 0.7 %maximum_select_fusion = f32[256,256]{1,0:T(8,128)} fusion(f32[128,256]{1,0:T(8,128)S(1)} %collective-permute-done.17, f32[128,256]{1,0:T(8,128)S(1)} %add_add_fusion, pred[]{:T(512)S(6)} %eq.5), kind=kLoop, calls=%fused_computation.4 | loop fusion | flops 196608 | bytes 524289 | tf_op jit(solution)/shard_map/jit(_where)/select_n | solution.py:209
  (37 shorter events, 0.8 us)
Async XLA Ops:
  0.6 37.6 %copy-start = (bf16[256,256]{1,0:T(8,128)(2,1)S(1)}, bf16[256,256]{1,0:T(8,128)(2,1)}, u32[]{:S(2)}) copy-start(bf16[256,256]{1,0:T(8,128)(2,1)} %param.11) | copy-start | bytes 393220
  0.6 14.3 %copy-start.1 = (bf16[128,256]{1,0:T(8,128)(2,1)S(1)}, bf16[128,256]{1,0:T(8,128)(2,1)}, u32[]{:S(2)}) copy-start(bf16[128,256]{1,0:T(8,128)(2,1)} %param.10) | copy-start | bytes 196612
  1.7 11.3 %collective-permute-start.1 = (bf16[128,256]{1,0:T(8,128)(2,1)S(1)}, bf16[128,256]{1,0:T(8,128)(2,1)S(1)}, u32[]{:S(2)}, u32[]{:S(2)}) collective-permute-start(bf16[128,256]{1,0:T(8,128)(2,1)S(1)} %convert_multiply_fusion), channel_id=1, source_target_pairs={{0,12},{1,13},{2,14},{3,15},{4,8},{5,9},{6,10},{7,11},{8,4},{9,5},... | collective-permute-start | bytes 196616 | tf_op jit(solution)/shard_map/ppermute | solution.py:62
  6.8 6.2 %collective-permute-start.2 = (bf16[128,256]{1,0:T(8,128)(2,1)S(1)}, bf16[128,256]{1,0:T(8,128)(2,1)S(1)}, u32[]{:S(2)}, u32[]{:S(2)}) collective-permute-start(bf16[128,256]{1,0:T(8,128)(2,1)S(1)} %convert_multiply_fusion), channel_id=1, source_target_pairs={{0,8},{1,9},{2,10},{3,11},{4,12},{5,13},{6,14},{7,15},{8,0},{9,1},... | collective-permute-start | bytes 196616 | tf_op jit(solution)/shard_map/ppermute | solution.py:62
  6.8 6.2 %collective-permute-start.3 = (bf16[128,256]{1,0:T(8,128)(2,1)S(1)}, bf16[128,256]{1,0:T(8,128)(2,1)S(1)}, u32[]{:S(2)}, u32[]{:S(2)}) collective-permute-start(bf16[128,256]{1,0:T(8,128)(2,1)S(1)} %convert_multiply_fusion), channel_id=1, source_target_pairs={{0,4},{1,5},{2,6},{3,7},{4,0},{5,1},{6,2},{7,3},{8,12},{9,13},{10,... | collective-permute-start | bytes 196616 | tf_op jit(solution)/shard_map/ppermute | solution.py:62
  7.4 5.6 %collective-permute-start = (bf16[128,256]{1,0:T(8,128)(2,1)}, bf16[128,256]{1,0:T(8,128)(2,1)S(1)}, u32[]{:S(2)}, u32[]{:S(2)}) collective-permute-start(bf16[128,256]{1,0:T(8,128)(2,1)} %param.10), channel_id=1, source_target_pairs={{0,16},{1,17},{2,18},{3,19},{4,20},{5,21},{6,22},{7,23},{8,24},{9,... | collective-permute-start | bytes 196616 | tf_op jit(solution)/shard_map/ppermute | solution.py:62
  13.0 7.4 %collective-permute-start.4 = (bf16[512,256]{1,0:T(8,128)(2,1)S(1)}, bf16[512,256]{1,0:T(8,128)(2,1)S(1)}, u32[]{:S(2)}, u32[]{:S(2)}) collective-permute-start(bf16[512,256]{1,0:T(8,128)(2,1)S(1)} %pad_maximum_fusion.2), channel_id=1, source_target_pairs={{0,2},{1,3},{2,0},{3,1},{4,6},{5,7},{6,4},{7,5},{8,10},{9,11},{10,... | collective-permute-start | bytes 786440 | tf_op jit(solution)/shard_map/ppermute | solution.py:62
  14.3 6.1 %collective-permute-start.6 = (bf16[128,1024]{1,0:T(8,128)(2,1)S(1)}, bf16[128,1024]{1,0:T(8,128)(2,1)S(1)}, u32[]{:S(2)}, u32[]{:S(2)}) collective-permute-start(bf16[128,1024]{1,0:T(8,128)(2,1)S(1)} %get-tuple-element.30), channel_id=1, source_target_pairs={{0,1},{1,0},{2,3},{3,2},{4,5},{5,4},{6,7},{7,6},{8,9},{9,8},{10,11... | collective-permute-start | bytes 786440 | tf_op jit(solution)/shard_map/ppermute | solution.py:62
  14.4 6.0 %collective-permute-start.7 = (bf16[128,1024]{1,0:T(8,128)(2,1)S(1)}, bf16[128,1024]{1,0:T(8,128)(2,1)S(1)}, u32[]{:S(2)}, u32[]{:S(2)}) collective-permute-start(bf16[128,1024]{1,0:T(8,128)(2,1)S(1)} %get-tuple-element.31), channel_id=1, source_target_pairs={{0,1},{1,0},{2,3},{3,2},{4,5},{5,4},{6,7},{7,6},{8,9},{9,8},{10,11... | collective-permute-start | bytes 786440 | tf_op jit(solution)/shard_map/ppermute | solution.py:62
  14.9 5.5 %collective-permute-start.5 = (bf16[256,256]{1,0:T(8,128)(2,1)S(1)}, bf16[256,256]{1,0:T(8,128)(2,1)S(1)}, u32[]{:S(2)}, u32[]{:S(2)}) collective-permute-start(bf16[256,256]{1,0:T(8,128)(2,1)S(1)} %constant_dynamic-update-slice_fusion.own_in_ref), channel_id=1, source_target_pairs={{0,1},{1,0},{2,3},{3,2},{4,5},{5,4},{6,7},{7,6},{8,9},{9,8},{10,11... | collective-permute-start | bytes 393224 | tf_op jit(solution)/shard_map/ppermute | solution.py:62
  21.2 1.9 %collective-permute-start.10 = (f32[128,256]{1,0:T(8,128)S(1)}, f32[128,256]{1,0:T(8,128)S(1)}, u32[]{:S(2)}, u32[]{:S(2)}) collective-permute-start(f32[128,256]{1,0:T(8,128)S(1)} %get-tuple-element.29), channel_id=1, source_target_pairs={{0,1},{1,0},{2,3},{3,2},{4,5},{5,4},{6,7},{7,6},{8,9},{9,8},{10,11... | collective-permute-start | bytes 393224 | tf_op jit(solution)/shard_map/ppermute | solution.py:62
  21.4 6.3 %collective-permute-start.8 = (bf16[256,256]{1,0:T(8,128)(2,1)S(1)}, bf16[256,256]{1,0:T(8,128)(2,1)S(1)}, u32[]{:S(2)}, u32[]{:S(2)}) collective-permute-start(bf16[256,256]{1,0:T(8,128)(2,1)S(1)} %pad_maximum_fusion.3), channel_id=1, source_target_pairs={{0,16},{1,17},{2,18},{3,19},{4,20},{5,21},{6,22},{7,23},{8,24},{9,... | collective-permute-start | bytes 393224 | tf_op jit(solution)/shard_map/ppermute | solution.py:62
  23.1 6.1 %collective-permute-start.11 = (bf16[128,256]{1,0:T(8,128)(2,1)S(1)}, bf16[128,256]{1,0:T(8,128)(2,1)S(1)}, u32[]{:S(2)}, u32[]{:S(2)}) collective-permute-start(bf16[128,256]{1,0:T(8,128)(2,1)S(1)} %add_convert_fusion.1), channel_id=1, source_target_pairs={{0,12},{1,19},{2,14},{3,17},{4,8},{5,23},{6,10},{7,21},{8,4},{9,27... | collective-permute-start | bytes 196616 | tf_op jit(solution)/shard_map/ppermute | solution.py:164
  25.9 5.2 %collective-permute-start.12 = (bf16[128,256]{1,0:T(8,128)(2,1)S(1)}, bf16[128,256]{1,0:T(8,128)(2,1)S(1)}, u32[]{:S(2)}, u32[]{:S(2)}) collective-permute-start(bf16[128,256]{1,0:T(8,128)(2,1)S(1)} %add_convert_fusion.1), channel_id=1, source_target_pairs={{0,8},{1,3},{2,10},{3,1},{4,12},{5,7},{6,14},{7,5},{8,0},{9,11},{1... | collective-permute-start | bytes 196616 | tf_op jit(solution)/shard_map/ppermute | solution.py:164
  25.9 5.2 %collective-permute-start.13 = (bf16[128,256]{1,0:T(8,128)(2,1)S(1)}, bf16[128,256]{1,0:T(8,128)(2,1)S(1)}, u32[]{:S(2)}, u32[]{:S(2)}) collective-permute-start(bf16[128,256]{1,0:T(8,128)(2,1)S(1)} %add_convert_fusion.1), channel_id=1, source_target_pairs={{0,4},{1,17},{2,6},{3,19},{4,0},{5,21},{6,2},{7,23},{8,12},{9,25},... | collective-permute-start | bytes 196616 | tf_op jit(solution)/shard_map/ppermute | solution.py:164
  31.1 5.2 %collective-permute-start.14 = (bf16[128,256]{1,0:T(8,128)(2,1)S(1)}, bf16[128,256]{1,0:T(8,128)(2,1)S(1)}, u32[]{:S(2)}, u32[]{:S(2)}) collective-permute-start(bf16[128,256]{1,0:T(8,128)(2,1)S(1)} %add_convert_fusion), channel_id=1, source_target_pairs={{0,18},{1,13},{2,16},{3,15},{4,22},{5,9},{6,20},{7,11},{8,26},{9,5... | collective-permute-start | bytes 196616 | tf_op jit(solution)/shard_map/ppermute | solution.py:164
  33.0 4.3 %collective-permute-start.15 = (bf16[128,256]{1,0:T(8,128)(2,1)S(1)}, bf16[128,256]{1,0:T(8,128)(2,1)S(1)}, u32[]{:S(2)}, u32[]{:S(2)}) collective-permute-start(bf16[128,256]{1,0:T(8,128)(2,1)S(1)} %add_convert_fusion), channel_id=1, source_target_pairs={{0,2},{1,9},{2,0},{3,11},{4,6},{5,13},{6,4},{7,15},{8,10},{9,1},{1... | collective-permute-start | bytes 196616 | tf_op jit(solution)/shard_map/ppermute | solution.py:164
  33.9 4.3 %collective-permute-start.16 = (bf16[128,256]{1,0:T(8,128)(2,1)S(1)}, bf16[128,256]{1,0:T(8,128)(2,1)S(1)}, u32[]{:S(2)}, u32[]{:S(2)}) collective-permute-start(bf16[128,256]{1,0:T(8,128)(2,1)S(1)} %add_convert_fusion), channel_id=1, source_target_pairs={{0,16},{1,5},{2,18},{3,7},{4,20},{5,1},{6,22},{7,3},{8,24},{9,13},... | collective-permute-start | bytes 196616 | tf_op jit(solution)/shard_map/ppermute | solution.py:164
  34.7 3.6 %collective-permute-start.9 = (bf16[128,256]{1,0:T(8,128)(2,1)S(1)}, bf16[128,256]{1,0:T(8,128)(2,1)S(1)}, u32[]{:S(2)}, u32[]{:S(2)}) collective-permute-start(bf16[128,256]{1,0:T(8,128)(2,1)S(1)} %fusion), channel_id=1, source_target_pairs={{0,1},{1,0},{2,3},{3,2},{4,5},{5,4},{6,7},{7,6},{8,9},{9,8},{10,11... | collective-permute-start | bytes 196616 | tf_op jit(solution)/shard_map/ppermute | solution.py:62
  38.2 1.4 %collective-permute-start.17 = (f32[128,256]{1,0:T(8,128)S(1)}, f32[128,256]{1,0:T(8,128)S(1)}, u32[]{:S(2)}, u32[]{:S(2)}) collective-permute-start(f32[128,256]{1,0:T(8,128)S(1)} %add_add_fusion), channel_id=1, source_target_pairs={{0,1},{1,0},{2,3},{3,2},{4,5},{5,4},{6,7},{7,6},{8,9},{9,8},{10,11... | collective-permute-start | bytes 393224 | tf_op jit(solution)/shard_map/ppermute | solution.py:62

commit v4 on v3

--- a/solution.py
+++ b/solution.py
@@ -62,12 +62,11 @@
     return lax.ppermute(value, both, [(i, i ^ mask) for i in range(total)])
 
 
-def merge_kernel(order, group, spots_ref, values_ref, *rest):
-    halves, (staged, sems), sums = rest[:2], rest[2:4], rest[4:]
+def merge_kernel(order, group, spots_in_ref, values_ref, *rest):
+    halves, (staged, spots_ref, sems, spots_sem), sums = rest[:2], rest[2:6], rest[6:]
     slots = values_ref.shape[0]
     sources = len(order)
     blk = values_ref.shape[1]
-    count = spots_ref[slots]
     pieces = slots // group
     ways = len(sums)
     spare = sums[0].shape[0] - 1
@@ -76,7 +75,13 @@
         part = pl.ds(i * group, group)
         return pltpu.make_async_copy(values_ref.at[part], staged.at[part], sems.at[i])
 
-    for i in range(pieces):
+    spots_copy = pltpu.make_async_copy(spots_in_ref, spots_ref, spots_sem)
+    spots_copy.start()
+    for i in range(2):
+        piece_copy(i).start()
+    spots_copy.wait()
+    count = spots_ref[slots]
+    for i in range(2, pieces):
         @pl.when(i * group < count)
         def _(i=i):
             piece_copy(i).start()
@@ -84,7 +89,7 @@
     for total in sums:
         total[...] = jnp.zeros_like(total)
     for i in range(pieces):
-        @pl.when(i * group < count)
+        @pl.when((i < 2) | (i * group < count))
         def _(i=i):
             piece_copy(i).wait()
 
@@ -115,11 +120,13 @@
     return pl.pallas_call(
         functools.partial(merge_kernel, order, group),
         out_shape=[half, half],
-        in_specs=[smem, pl.BlockSpec(memory_space=pltpu.HBM)],
+        in_specs=[pl.BlockSpec(memory_space=pl.ANY), pl.BlockSpec(memory_space=pltpu.HBM)],
         out_specs=[vmem, vmem],
         scratch_shapes=[
             pltpu.VMEM(values.shape, values.dtype),
+            pltpu.SMEM(spots.shape, spots.dtype),
             pltpu.SemaphoreType.DMA((slots // group,)),
+            pltpu.SemaphoreType.DMA,
         ] + [pltpu.VMEM((out_blocks * len(order) + 1, blk, blk), jnp.float32)] * ways,
         compiler_params=pltpu.CompilerParams(vmem_limit_bytes=50 * 1024 * 1024),
         cost_estimate=pl.CostEstimate(flops=slots * blk * blk, bytes_accessed=4 * slots * blk * blk, transcendentals=0),
@@ -138,7 +145,7 @@
     rows = terms.shape[0] // 2
     upper = place_ref[0] == 0
     keep_ref[...] = jnp.where(upper, terms[:rows], terms[rows:])
-    send_ref[...] = jnp.where(upper, terms[rows:], terms[:rows])
+    send_ref[...] = jnp.where(upper, terms[rows:], terms[:rows]).astype(send_ref.dtype)
 
 
 def products(place, own_tiles, twin_tiles, near, own_in, twin_in, scale):
@@ -149,7 +156,7 @@
         functools.partial(product_kernel, scale),
         out_shape=[
             jax.ShapeDtypeStruct(part, jnp.float32),
-            jax.ShapeDtypeStruct(part, jnp.float32),
+            jax.ShapeDtypeStruct(part, jnp.bfloat16),
             jax.ShapeDtypeStruct((rows, features), jnp.float32),
             jax.ShapeDtypeStruct((rows, features), jnp.bfloat16),
         ],

time: 40.4 us -> 40.3 us (level)
  starting transfers between devices: 19.3 us -> 20.4 us
  waiting for transfers between devices: 12.6 us -> 12 us
  Pallas kernels: 3.29 us -> 2.82 us
    ppermute x6, waiting for transfers between devices: 6.77 us -> 5.37 us  [core_swap(): lax.ppermute(value, both, [(i, i ^ masks[i % 2]) for i in range(total)])]
    ppermute x12, waiting for transfers between devices: 5.82 us -> 6.64 us  [swap(): return lax.ppermute(value, both, [(i, i ^ mask) for i in range(total)])]
    ppermute x12, starting transfers between devices: 11.3 us -> 12.1 us  [swap(): return lax.ppermute(value, both, [(i, i ^ mask) for i in range(total)])]
    pallas_call x1, Pallas kernels: 2.53 us -> 2.06 us  [merge_tiles(): pl.pallas_call(functools.partial(merge_kernel, order, group), out_shape=[...]
  transfers between devices with their start and end apart: 18 -> 18, of which waited for: 7 -> 7; matrix products, arithmetic and copies ran while one was open for 4% -> 4% of each run, Pallas kernels for 6% -> 5%
where the time goes in v4:
time: 40.3 us
  starting transfers between devices  20.4 us (51%)
  waiting for transfers between devices  12 us (30%)
  Pallas kernels  2.82 us (7%)
  other arithmetic  2.63 us (7%)
  between operations  1.52 us (4%)
  matrix products  0.84 us (2%)
    ppermute x12, starting transfers between devices, swap(): return lax.ppermute(value, both, [(i, i ^ mask) for i in range(total)])  12.1 us
    ppermute x6, starting transfers between devices, core_swap(): lax.ppermute(value, both, [(i, i ^ masks[i % 2]) for i in range(total)])  8.27 us
    ppermute x12, waiting for transfers between devices, swap(): return lax.ppermute(value, both, [(i, i ^ mask) for i in range(total)])  6.64 us
    ppermute x6, waiting for transfers between devices, core_swap(): lax.ppermute(value, both, [(i, i ^ masks[i % 2]) for i in range(total)])  5.37 us
    pallas_call x1, Pallas kernels, merge_tiles(): pl.pallas_call(functools.partial(merge_kernel, order, group), out_shape=[...  2.06 us
    mul x1, other arithmetic, pair_body(): masked = grad_out * relu_mask.astype(jnp.bfloat16)  1 us
    dot_general x1, matrix products, pair_body(): lax.dot_general(prop, weight, (((1,), (1,)), ((), ())), preferred_element...  0.84 us
  transfers between devices with their start and end apart: 18, of which 7 were waited for; matrix products, arithmetic and copies ran while one was open for 4% of the time, Pallas kernels for 5%

profile of v4, /device:TPU:0, one launch (start us, length us, event | category | flops | bytes accessed | tf_op | source)
XLA Modules:
  0.0 40.3 jit_solution(15685161935871529230)
XLA Ops:
  0.7 1.0 %convert_multiply_fusion = bf16[128,256]{1,0:T(8,128)(2,1)S(1)} fusion(bf16[128,256]{1,0:T(8,128)(2,1)} %param.8, s32[128,256]{1,0:T(8,128)} %param.9), kind=kLoop, calls=%fused_computation.15 | loop fusion | flops 65536 | bytes 262144 | tf_op jit(solution)/shard_map/mul | solution.py:186
  1.7 5.1 %collective-permute-start.1 = (bf16[128,256]{1,0:T(8,128)(2,1)S(1)}, bf16[128,256]{1,0:T(8,128)(2,1)S(1)}, u32[]{:S(2)}, u32[]{:S(2)}) collective-permute-start(bf16[128,256]{1,0:T(8,128)(2,1)S(1)} %convert_multiply_fusion), channel_id=1, source_target_pairs={{0,12},{1,13},{2,14},{3,15},{4,8},{5,9},{6,10},{7,11},{8,4},{9,5},... | collective-permute-start | bytes 196616 | tf_op jit(solution)/shard_map/ppermute | solution.py:62
  6.8 0.6 %collective-permute-start.3 = (bf16[128,256]{1,0:T(8,128)(2,1)S(1)}, bf16[128,256]{1,0:T(8,128)(2,1)S(1)}, u32[]{:S(2)}, u32[]{:S(2)}) collective-permute-start(bf16[128,256]{1,0:T(8,128)(2,1)S(1)} %convert_multiply_fusion), channel_id=1, source_target_pairs={{0,4},{1,5},{2,6},{3,7},{4,0},{5,1},{6,2},{7,3},{8,12},{9,13},{10,... | collective-permute-start | bytes 196616 | tf_op jit(solution)/shard_map/ppermute | solution.py:62
  7.4 1.6 %collective-permute-start = (bf16[128,256]{1,0:T(8,128)(2,1)}, bf16[128,256]{1,0:T(8,128)(2,1)S(1)}, u32[]{:S(2)}, u32[]{:S(2)}) collective-permute-start(bf16[128,256]{1,0:T(8,128)(2,1)} %param.10), channel_id=1, source_target_pairs={{0,16},{1,17},{2,18},{3,19},{4,20},{5,21},{6,22},{7,23},{8,24},{9,... | collective-permute-start | bytes 196616 | tf_op jit(solution)/shard_map/ppermute | solution.py:62
  9.7 0.7 %xor_add_fusion = s32[128]{0:T(128)S(1)} fusion(s32[128]{0:T(128)} %param.14, s32[128]{0:T(128)} %param.13, s32[]{:T(128)S(6)} %axis_index.22, s32[]{:T(128)S(6)} %axis_index.25), kind=kLoop, calls=%fused_computation.19 | loop fusion | flops 512 | bytes 1544 | tf_op jit(solution)/shard_map/add | solution.py:194
  10.4 2.1 %shard_map.95 = (bf16[256,1024]{1,0:T(8,128)(2,1)S(1)}, bf16[256,1024]{1,0:T(8,128)(2,1)S(1)}) custom-call(s32[129]{0:T(256)S(1)} %pad_add_fusion.spots_in_ref, bf16[128,128,128]{2,1,0:T(8,128)(2,1)} %values_ref.1), custom_call_target="tpu_custom_call" | custom-call | flops 2097152 | bytes 8388608 | tf_op jit(solution)/shard_map/pallas_call | solution.py:120
  12.5 2.1 %collective-permute-start.4 = (bf16[512,256]{1,0:T(8,128)(2,1)S(1)}, bf16[512,256]{1,0:T(8,128)(2,1)S(1)}, u32[]{:S(2)}, u32[]{:S(2)}) collective-permute-start(bf16[512,256]{1,0:T(8,128)(2,1)S(1)} %pad_maximum_fusion.2), channel_id=1, source_target_pairs={{0,2},{1,3},{2,0},{3,1},{4,6},{5,7},{6,4},{7,5},{8,10},{9,11},{10,... | collective-permute-start | bytes 786440 | tf_op jit(solution)/shard_map/ppermute | solution.py:62
  14.7 0.5 %collective-permute-start.7 = (bf16[128,1024]{1,0:T(8,128)(2,1)S(1)}, bf16[128,1024]{1,0:T(8,128)(2,1)S(1)}, u32[]{:S(2)}, u32[]{:S(2)}) collective-permute-start(bf16[128,1024]{1,0:T(8,128)(2,1)S(1)} %get-tuple-element.31), channel_id=1, source_target_pairs={{0,1},{1,0},{2,3},{3,2},{4,5},{5,4},{6,7},{7,6},{8,9},{9,8},{10,11... | collective-permute-start | bytes 786440 | tf_op jit(solution)/shard_map/ppermute | solution.py:62
  15.4 4.9 %collective-permute-done.4 = bf16[512,256]{1,0:T(8,128)(2,1)S(1)} collective-permute-done((bf16[512,256]{1,0:T(8,128)(2,1)S(1)}, bf16[512,256]{1,0:T(8,128)(2,1)S(1)}, u32[]{:S(2)}, u32[]{:S(2)}) %collective-permute-start.4) | collective-permute-done | bytes 262176 | tf_op jit(solution)/shard_map/ppermute | solution.py:62
  20.5 0.8 %shard_map.96 = (f32[128,256]{1,0:T(8,128)S(1)}, bf16[128,256]{1,0:T(8,128)(2,1)S(1)}, f32[256,256]{1,0:T(8,128)S(1)}, bf16[256,256]{1,0:T(8,128)(2,1)S(1)}) custom-call(s32[1]{0:T(128)} %bitcast.place_ref, bf16[256,1024]{1,0:T(8,128)(2,1)S(1)} %get-tuple-element.18.own_tiles_ref, bf16[256,1024]{1,0:T(8,128)(2,1)S(1)} %pad_maximum_fusion.1.twin_tiles_ref, ...), custom_call_target="tpu_custom_call" | custom-call | flops 268435456 | bytes 1048576 | tf_op jit(solution)/shard_map/pallas_call | solution.py:155
  21.4 1.2 %collective-permute-done.10 = bf16[128,256]{1,0:T(8,128)(2,1)S(1)} collective-permute-done((bf16[128,256]{1,0:T(8,128)(2,1)S(1)}, bf16[128,256]{1,0:T(8,128)(2,1)S(1)}, u32[]{:S(2)}, u32[]{:S(2)}) %collective-permute-start.10) | collective-permute-done | bytes 65568 | tf_op jit(solution)/shard_map/ppermute | solution.py:62
  22.6 3.5 %collective-permute-start.11 = (bf16[128,256]{1,0:T(8,128)(2,1)S(1)}, bf16[128,256]{1,0:T(8,128)(2,1)S(1)}, u32[]{:S(2)}, u32[]{:S(2)}) collective-permute-start(bf16[128,256]{1,0:T(8,128)(2,1)S(1)} %add_convert_fusion.1), channel_id=1, source_target_pairs={{0,12},{1,19},{2,14},{3,17},{4,8},{5,23},{6,10},{7,21},{8,4},{9,27... | collective-permute-start | bytes 196616 | tf_op jit(solution)/shard_map/ppermute | solution.py:171
  26.1 1.0 %collective-permute-start.13 = (bf16[128,256]{1,0:T(8,128)(2,1)S(1)}, bf16[128,256]{1,0:T(8,128)(2,1)S(1)}, u32[]{:S(2)}, u32[]{:S(2)}) collective-permute-start(bf16[128,256]{1,0:T(8,128)(2,1)S(1)} %add_convert_fusion.1), channel_id=1, source_target_pairs={{0,4},{1,17},{2,6},{3,19},{4,0},{5,21},{6,2},{7,23},{8,12},{9,25},... | collective-permute-start | bytes 196616 | tf_op jit(solution)/shard_map/ppermute | solution.py:171
  27.1 1.7 %collective-permute-start.8 = (bf16[256,256]{1,0:T(8,128)(2,1)S(1)}, bf16[256,256]{1,0:T(8,128)(2,1)S(1)}, u32[]{:S(2)}, u32[]{:S(2)}) collective-permute-start(bf16[256,256]{1,0:T(8,128)(2,1)S(1)} %pad_maximum_fusion.3), channel_id=1, source_target_pairs={{0,16},{1,17},{2,18},{3,19},{4,20},{5,21},{6,22},{7,23},{8,24},{9,... | collective-permute-start | bytes 393224 | tf_op jit(solution)/shard_map/ppermute | solution.py:62
  28.8 2.6 %collective-permute-done.12 = bf16[128,256]{1,0:T(8,128)(2,1)S(1)} collective-permute-done((bf16[128,256]{1,0:T(8,128)(2,1)S(1)}, bf16[128,256]{1,0:T(8,128)(2,1)S(1)}, u32[]{:S(2)}, u32[]{:S(2)}) %collective-permute-start.12) | collective-permute-done | bytes 65568 | tf_op jit(solution)/shard_map/ppermute | solution.py:171
  31.4 1.5 %collective-permute-start.14 = (bf16[128,256]{1,0:T(8,128)(2,1)S(1)}, bf16[128,256]{1,0:T(8,128)(2,1)S(1)}, u32[]{:S(2)}, u32[]{:S(2)}) collective-permute-start(bf16[128,256]{1,0:T(8,128)(2,1)S(1)} %add_convert_fusion), channel_id=1, source_target_pairs={{0,18},{1,13},{2,16},{3,15},{4,22},{5,9},{6,20},{7,11},{8,26},{9,5... | collective-permute-start | bytes 196616 | tf_op jit(solution)/shard_map/ppermute | solution.py:171
  32.9 1.0 %collective-permute-start.15 = (bf16[128,256]{1,0:T(8,128)(2,1)S(1)}, bf16[128,256]{1,0:T(8,128)(2,1)S(1)}, u32[]{:S(2)}, u32[]{:S(2)}) collective-permute-start(bf16[128,256]{1,0:T(8,128)(2,1)S(1)} %add_convert_fusion), channel_id=1, source_target_pairs={{0,2},{1,9},{2,0},{3,11},{4,6},{5,13},{6,4},{7,15},{8,10},{9,1},{1... | collective-permute-start | bytes 196616 | tf_op jit(solution)/shard_map/ppermute | solution.py:171
  33.8 1.4 %collective-permute-start.16 = (bf16[128,256]{1,0:T(8,128)(2,1)S(1)}, bf16[128,256]{1,0:T(8,128)(2,1)S(1)}, u32[]{:S(2)}, u32[]{:S(2)}) collective-permute-start(bf16[128,256]{1,0:T(8,128)(2,1)S(1)} %add_convert_fusion), channel_id=1, source_target_pairs={{0,16},{1,5},{2,18},{3,7},{4,20},{5,1},{6,22},{7,3},{8,24},{9,13},... | collective-permute-start | bytes 196616 | tf_op jit(solution)/shard_map/ppermute | solution.py:171
  35.3 1.3 %collective-permute-done.14 = bf16[128,256]{1,0:T(8,128)(2,1)S(1)} collective-permute-done((bf16[128,256]{1,0:T(8,128)(2,1)S(1)}, bf16[128,256]{1,0:T(8,128)(2,1)S(1)}, u32[]{:S(2)}, u32[]{:S(2)}) %collective-permute-start.14) | collective-permute-done | bytes 65568 | tf_op jit(solution)/shard_map/ppermute | solution.py:171
  36.6 0.7 %collective-permute-done.15 = bf16[128,256]{1,0:T(8,128)(2,1)S(1)} collective-permute-done((bf16[128,256]{1,0:T(8,128)(2,1)S(1)}, bf16[128,256]{1,0:T(8,128)(2,1)S(1)}, u32[]{:S(2)}, u32[]{:S(2)}) %collective-permute-start.15) | collective-permute-done | bytes 65568 | tf_op jit(solution)/shard_map/ppermute | solution.py:171
  37.3 0.8 %collective-permute-done.16 = bf16[128,256]{1,0:T(8,128)(2,1)S(1)} collective-permute-done((bf16[128,256]{1,0:T(8,128)(2,1)S(1)}, bf16[128,256]{1,0:T(8,128)(2,1)S(1)}, u32[]{:S(2)}, u32[]{:S(2)}) %collective-permute-start.16) | collective-permute-done | bytes 65568 | tf_op jit(solution)/shard_map/ppermute | solution.py:171
  38.3 0.8 %convolution_convert_fusion = bf16[128,256]{1,0:T(8,128)(2,1)} fusion(bf16[256,256]{1,0:T(8,128)(2,1)S(1)} %copy-done, f32[256,256]{1,0:T(8,128)S(1)} %convert_element_type.56, bf16[128,256]{1,0:T(8,128)(2,1)S(1)} %collective-permute-done.9, f32[256,256]{1,0:T(8,128)S(1)} %get-tuple-element.26), kind=kOutput, calls=%fused_computation | convolution fusion | flops 16941056 | bytes 524288 | tf_op jit(solution)/shard_map/dot_general | solution.py:222
  39.1 0.5 %collective-permute-done.17 = f32[128,256]{1,0:T(8,128)S(1)} collective-permute-done((f32[128,256]{1,0:T(8,128)S(1)}, f32[128,256]{1,0:T(8,128)S(1)}, u32[]{:S(2)}, u32[]{:S(2)}) %collective-permute-start.17) | collective-permute-done | bytes 131104 | tf_op jit(solution)/shard_map/ppermute | solution.py:62
  39.6 0.7 %maximum_select_fusion = f32[256,256]{1,0:T(8,128)} fusion(f32[128,256]{1,0:T(8,128)S(1)} %collective-permute-done.17, f32[128,256]{1,0:T(8,128)S(1)} %add_add_fusion, pred[]{:T(512)S(6)} %eq.5), kind=kLoop, calls=%fused_computation.4 | loop fusion | flops 196608 | bytes 524289 | tf_op jit(solution)/shard_map/jit(_where)/select_n | solution.py:216
  (37 shorter events, 0.8 us)
Async XLA Ops:
  0.6 37.6 %copy-start = (bf16[256,256]{1,0:T(8,128)(2,1)S(1)}, bf16[256,256]{1,0:T(8,128)(2,1)}, u32[]{:S(2)}) copy-start(bf16[256,256]{1,0:T(8,128)(2,1)} %param.11) | copy-start | bytes 393220
  0.6 14.6 %copy-start.1 = (bf16[128,256]{1,0:T(8,128)(2,1)S(1)}, bf16[128,256]{1,0:T(8,128)(2,1)}, u32[]{:S(2)}) copy-start(bf16[128,256]{1,0:T(8,128)(2,1)} %param.10) | copy-start | bytes 196612
  1.7 10.8 %collective-permute-start.1 = (bf16[128,256]{1,0:T(8,128)(2,1)S(1)}, bf16[128,256]{1,0:T(8,128)(2,1)S(1)}, u32[]{:S(2)}, u32[]{:S(2)}) collective-permute-start(bf16[128,256]{1,0:T(8,128)(2,1)S(1)} %convert_multiply_fusion), channel_id=1, source_target_pairs={{0,12},{1,13},{2,14},{3,15},{4,8},{5,9},{6,10},{7,11},{8,4},{9,5},... | collective-permute-start | bytes 196616 | tf_op jit(solution)/shard_map/ppermute | solution.py:62
  6.8 5.7 %collective-permute-start.2 = (bf16[128,256]{1,0:T(8,128)(2,1)S(1)}, bf16[128,256]{1,0:T(8,128)(2,1)S(1)}, u32[]{:S(2)}, u32[]{:S(2)}) collective-permute-start(bf16[128,256]{1,0:T(8,128)(2,1)S(1)} %convert_multiply_fusion), channel_id=1, source_target_pairs={{0,8},{1,9},{2,10},{3,11},{4,12},{5,13},{6,14},{7,15},{8,0},{9,1},... | collective-permute-start | bytes 196616 | tf_op jit(solution)/shard_map/ppermute | solution.py:62
  6.8 5.7 %collective-permute-start.3 = (bf16[128,256]{1,0:T(8,128)(2,1)S(1)}, bf16[128,256]{1,0:T(8,128)(2,1)S(1)}, u32[]{:S(2)}, u32[]{:S(2)}) collective-permute-start(bf16[128,256]{1,0:T(8,128)(2,1)S(1)} %convert_multiply_fusion), channel_id=1, source_target_pairs={{0,4},{1,5},{2,6},{3,7},{4,0},{5,1},{6,2},{7,3},{8,12},{9,13},{10,... | collective-permute-start | bytes 196616 | tf_op jit(solution)/shard_map/ppermute | solution.py:62
  7.4 5.1 %collective-permute-start = (bf16[128,256]{1,0:T(8,128)(2,1)}, bf16[128,256]{1,0:T(8,128)(2,1)S(1)}, u32[]{:S(2)}, u32[]{:S(2)}) collective-permute-start(bf16[128,256]{1,0:T(8,128)(2,1)} %param.10), channel_id=1, source_target_pairs={{0,16},{1,17},{2,18},{3,19},{4,20},{5,21},{6,22},{7,23},{8,24},{9,... | collective-permute-start | bytes 196616 | tf_op jit(solution)/shard_map/ppermute | solution.py:62
  12.5 7.8 %collective-permute-start.4 = (bf16[512,256]{1,0:T(8,128)(2,1)S(1)}, bf16[512,256]{1,0:T(8,128)(2,1)S(1)}, u32[]{:S(2)}, u32[]{:S(2)}) collective-permute-start(bf16[512,256]{1,0:T(8,128)(2,1)S(1)} %pad_maximum_fusion.2), channel_id=1, source_target_pairs={{0,2},{1,3},{2,0},{3,1},{4,6},{5,7},{6,4},{7,5},{8,10},{9,11},{10,... | collective-permute-start | bytes 786440 | tf_op jit(solution)/shard_map/ppermute | solution.py:62
  14.7 5.7 %collective-permute-start.6 = (bf16[128,1024]{1,0:T(8,128)(2,1)S(1)}, bf16[128,1024]{1,0:T(8,128)(2,1)S(1)}, u32[]{:S(2)}, u32[]{:S(2)}) collective-permute-start(bf16[128,1024]{1,0:T(8,128)(2,1)S(1)} %get-tuple-element.30), channel_id=1, source_target_pairs={{0,1},{1,0},{2,3},{3,2},{4,5},{5,4},{6,7},{7,6},{8,9},{9,8},{10,11... | collective-permute-start | bytes 786440 | tf_op jit(solution)/shard_map/ppermute | solution.py:62
  14.7 5.7 %collective-permute-start.7 = (bf16[128,1024]{1,0:T(8,128)(2,1)S(1)}, bf16[128,1024]{1,0:T(8,128)(2,1)S(1)}, u32[]{:S(2)}, u32[]{:S(2)}) collective-permute-start(bf16[128,1024]{1,0:T(8,128)(2,1)S(1)} %get-tuple-element.31), channel_id=1, source_target_pairs={{0,1},{1,0},{2,3},{3,2},{4,5},{5,4},{6,7},{7,6},{8,9},{9,8},{10,11... | collective-permute-start | bytes 786440 | tf_op jit(solution)/shard_map/ppermute | solution.py:62
  15.3 5.2 %collective-permute-start.5 = (bf16[256,256]{1,0:T(8,128)(2,1)S(1)}, bf16[256,256]{1,0:T(8,128)(2,1)S(1)}, u32[]{:S(2)}, u32[]{:S(2)}) collective-permute-start(bf16[256,256]{1,0:T(8,128)(2,1)S(1)} %constant_dynamic-update-slice_fusion.own_in_ref), channel_id=1, source_target_pairs={{0,1},{1,0},{2,3},{3,2},{4,5},{5,4},{6,7},{7,6},{8,9},{9,8},{10,11... | collective-permute-start | bytes 393224 | tf_op jit(solution)/shard_map/ppermute | solution.py:62
  21.2 1.3 %collective-permute-start.10 = (bf16[128,256]{1,0:T(8,128)(2,1)S(1)}, bf16[128,256]{1,0:T(8,128)(2,1)S(1)}, u32[]{:S(2)}, u32[]{:S(2)}) collective-permute-start(bf16[128,256]{1,0:T(8,128)(2,1)S(1)} %get-tuple-element.29), channel_id=1, source_target_pairs={{0,1},{1,0},{2,3},{3,2},{4,5},{5,4},{6,7},{7,6},{8,9},{9,8},{10,11... | collective-permute-start | bytes 196616 | tf_op jit(solution)/shard_map/ppermute | solution.py:62
  22.6 6.2 %collective-permute-start.11 = (bf16[128,256]{1,0:T(8,128)(2,1)S(1)}, bf16[128,256]{1,0:T(8,128)(2,1)S(1)}, u32[]{:S(2)}, u32[]{:S(2)}) collective-permute-start(bf16[128,256]{1,0:T(8,128)(2,1)S(1)} %add_convert_fusion.1), channel_id=1, source_target_pairs={{0,12},{1,19},{2,14},{3,17},{4,8},{5,23},{6,10},{7,21},{8,4},{9,27... | collective-permute-start | bytes 196616 | tf_op jit(solution)/shard_map/ppermute | solution.py:171
  26.1 5.3 %collective-permute-start.12 = (bf16[128,256]{1,0:T(8,128)(2,1)S(1)}, bf16[128,256]{1,0:T(8,128)(2,1)S(1)}, u32[]{:S(2)}, u32[]{:S(2)}) collective-permute-start(bf16[128,256]{1,0:T(8,128)(2,1)S(1)} %add_convert_fusion.1), channel_id=1, source_target_pairs={{0,8},{1,3},{2,10},{3,1},{4,12},{5,7},{6,14},{7,5},{8,0},{9,11},{1... | collective-permute-start | bytes 196616 | tf_op jit(solution)/shard_map/ppermute | solution.py:171
  26.1 5.3 %collective-permute-start.13 = (bf16[128,256]{1,0:T(8,128)(2,1)S(1)}, bf16[128,256]{1,0:T(8,128)(2,1)S(1)}, u32[]{:S(2)}, u32[]{:S(2)}) collective-permute-start(bf16[128,256]{1,0:T(8,128)(2,1)S(1)} %add_convert_fusion.1), channel_id=1, source_target_pairs={{0,4},{1,17},{2,6},{3,19},{4,0},{5,21},{6,2},{7,23},{8,12},{9,25},... | collective-permute-start | bytes 196616 | tf_op jit(solution)/shard_map/ppermute | solution.py:171
  27.1 8.2 %collective-permute-start.8 = (bf16[256,256]{1,0:T(8,128)(2,1)S(1)}, bf16[256,256]{1,0:T(8,128)(2,1)S(1)}, u32[]{:S(2)}, u32[]{:S(2)}) collective-permute-start(bf16[256,256]{1,0:T(8,128)(2,1)S(1)} %pad_maximum_fusion.3), channel_id=1, source_target_pairs={{0,16},{1,17},{2,18},{3,19},{4,20},{5,21},{6,22},{7,23},{8,24},{9,... | collective-permute-start | bytes 393224 | tf_op jit(solution)/shard_map/ppermute | solution.py:62
  31.4 5.2 %collective-permute-start.14 = (bf16[128,256]{1,0:T(8,128)(2,1)S(1)}, bf16[128,256]{1,0:T(8,128)(2,1)S(1)}, u32[]{:S(2)}, u32[]{:S(2)}) collective-permute-start(bf16[128,256]{1,0:T(8,128)(2,1)S(1)} %add_convert_fusion), channel_id=1, source_target_pairs={{0,18},{1,13},{2,16},{3,15},{4,22},{5,9},{6,20},{7,11},{8,26},{9,5... | collective-permute-start | bytes 196616 | tf_op jit(solution)/shard_map/ppermute | solution.py:171
  32.9 4.5 %collective-permute-start.15 = (bf16[128,256]{1,0:T(8,128)(2,1)S(1)}, bf16[128,256]{1,0:T(8,128)(2,1)S(1)}, u32[]{:S(2)}, u32[]{:S(2)}) collective-permute-start(bf16[128,256]{1,0:T(8,128)(2,1)S(1)} %add_convert_fusion), channel_id=1, source_target_pairs={{0,2},{1,9},{2,0},{3,11},{4,6},{5,13},{6,4},{7,15},{8,10},{9,1},{1... | collective-permute-start | bytes 196616 | tf_op jit(solution)/shard_map/ppermute | solution.py:171
  33.8 4.3 %collective-permute-start.16 = (bf16[128,256]{1,0:T(8,128)(2,1)S(1)}, bf16[128,256]{1,0:T(8,128)(2,1)S(1)}, u32[]{:S(2)}, u32[]{:S(2)}) collective-permute-start(bf16[128,256]{1,0:T(8,128)(2,1)S(1)} %add_convert_fusion), channel_id=1, source_target_pairs={{0,16},{1,5},{2,18},{3,7},{4,20},{5,1},{6,22},{7,3},{8,24},{9,13},... | collective-permute-start | bytes 196616 | tf_op jit(solution)/shard_map/ppermute | solution.py:171
  35.3 3.0 %collective-permute-start.9 = (bf16[128,256]{1,0:T(8,128)(2,1)S(1)}, bf16[128,256]{1,0:T(8,128)(2,1)S(1)}, u32[]{:S(2)}, u32[]{:S(2)}) collective-permute-start(bf16[128,256]{1,0:T(8,128)(2,1)S(1)} %fusion), channel_id=1, source_target_pairs={{0,1},{1,0},{2,3},{3,2},{4,5},{5,4},{6,7},{7,6},{8,9},{9,8},{10,11... | collective-permute-start | bytes 196616 | tf_op jit(solution)/shard_map/ppermute | solution.py:62
  38.2 1.4 %collective-permute-start.17 = (f32[128,256]{1,0:T(8,128)S(1)}, f32[128,256]{1,0:T(8,128)S(1)}, u32[]{:S(2)}, u32[]{:S(2)}) collective-permute-start(f32[128,256]{1,0:T(8,128)S(1)} %add_add_fusion), channel_id=1, source_target_pairs={{0,1},{1,0},{2,3},{3,2},{4,5},{5,4},{6,7},{7,6},{8,9},{9,8},{10,11... | collective-permute-start | bytes 393224 | tf_op jit(solution)/shard_map/ppermute | solution.py:62
